TPU v7x, 32 devices: a whole 2x2x4 slice. The times are simulated.
32 devices in a mesh: groups: 2 (over y), replica: 4 (over z), tensor: 4 (over x, core).
Axes of the slice: x: 2, y: 2, z: 4, core: 2. Of those that a mesh axis runs over, the one named last changes fastest.
Arguments:
- ssm_state: bfloat16 [64, 64, 64, 128], P(('groups', 'replica'), 'tensor'), parts along dimension 0, may hold values from -6 to 6
- conv_state: bfloat16 [64, 3, 4, 1280], P(('groups', 'replica'), None, 'tensor'), parts along dimension 0, may hold values from -6 to 6
- dst_replica: int32 [64], P(('groups', 'replica')), parts along dimension 0, may hold values from 0 to 3, as said below
- dst_slot: int32 [64], P(('groups', 'replica')), parts along dimension 0, may hold values from 0 to 7, as said below
- live: int32 [8], P('groups'), parts along dimension 0, may hold values from 1 to 8, as said below
- conv_in: bfloat16 [2, 64, 4, 1280], P(None, ('groups', 'replica'), 'tensor'), parts along dimension 1, may hold values from -6 to 6
- gate_in: bfloat16 [2, 64, 4096], P(None, ('groups', 'replica'), 'tensor'), parts along dimension 1, may hold values from -6 to 6
- dt_in: bfloat16 [2, 64, 64], P(None, ('groups', 'replica'), 'tensor'), parts along dimension 1, may hold values from -6 to 6
- conv_weight: bfloat16 [4, 4, 1280], P(None, 'tensor'), may hold values from -3 to 3
- conv_bias: bfloat16 [4, 1280], P('tensor'), may hold values from -3 to 3
- dt_bias: float32 [64], P('tensor'), may hold values from -4.6 to -2.3
- a_log: float32 [64], P('tensor'), may hold values from 0 to 2.77
- skip_gain: float32 [64], P('tensor'), may hold values from 0.5 to 2
- norm_gain: bfloat16 [4096], P('tensor'), may hold values from 0.099609375 to 1.8984375
- out_weight: bfloat16 [4096, 4096], P('tensor'), may hold values from -0.09375 to 0.09375
Outputs:
- mixed: bfloat16 [2, 64, 4096], P(None, ('groups', 'replica')), parts along dimension 1
- ssm_after: bfloat16 [64, 64, 64, 128], P(('groups', 'replica'), 'tensor'), parts along dimension 0
- conv_after: bfloat16 [64, 3, 4, 1280], P(('groups', 'replica'), None, 'tensor'), parts along dimension 0
There are 2 independent parts, one for each index of `groups`. A program takes and returns all parts, laid end to end along the dimension named above; an argument that names none is the same for every part. Nothing has to cross between parts.
Inputs may be any that keep to these rules, and one draw needn't show every extreme that they name: `dst_replica`: the 8 requests of one replica go to 2 different replicas, exactly 4 to each; every replica receives exactly 8 requests. (dst_replica, dst_slot) differs between requests, so every slot of every replica receives one request. Some replica has all 8 slots live.
All inputs are finite; a program needn't handle non-finite values.
Results may differ from a plain program's by a relative error of at most 0.0049.
Values may be sent and summed in bfloat16 or wider, within the bound.
No kernel may reach another device: no remote copies, remote signals or barrier semaphores. Data moves between devices by JAX's collectives and lax.ppermute only.
A program may use at most 128 MiB of HBM per device.

v0:
```python
import jax
import jax.numpy as jnp
from jax import lax
from jax.sharding import PartitionSpec as P

HEADS = 64
GROUPS = 4


def convolve(window_rows, conv_tokens, conv_weight, conv_bias):
    weight_rows = conv_weight.astype(jnp.float32)
    shift_rows = conv_bias.astype(jnp.float32)
    activations = []
    for step_index in range(conv_tokens.shape[0]):
        stacked = jnp.concatenate([window_rows, conv_tokens[step_index][:, None]], axis=1)
        summed = jnp.sum(stacked.astype(jnp.float32) * weight_rows[None], axis=1) + shift_rows
        activations.append(jax.nn.silu(summed))
        window_rows = stacked[:, 1:]
    return (activations, window_rows)


def advance(
    states_now,
    activations,
    dt_tokens,
    gate_tokens,
    dt_bias,
    a_log,
    skip_gain,
    norm_gain,
    heads_per_group,
):
    decay_rate = -jnp.exp(a_log)
    row_count, head_count, head_width, state_width = states_now.shape
    group_span = heads_per_group * head_width
    normed_list = []
    for step_index in range(len(activations)):
        act_rows = activations[step_index]
        group_count = act_rows.shape[1]
        values = act_rows[..., :group_span].reshape(row_count, head_count, head_width)
        input_map = jnp.repeat(
            act_rows[..., group_span : group_span + state_width], heads_per_group, axis=1
        )
        output_map = jnp.repeat(act_rows[..., group_span + state_width :], heads_per_group, axis=1)
        step_size = jax.nn.softplus(dt_tokens[step_index].astype(jnp.float32) + dt_bias)
        retained = jnp.exp(step_size * decay_rate)
        states_now = (
            retained[:, :, None, None] * states_now
            + (step_size[:, :, None] * values)[:, :, :, None] * input_map[:, :, None, :]
        )
        readout = (
            jnp.einsum("shpn,shn->shp", states_now, output_map, precision=lax.Precision.HIGHEST)
            + skip_gain[None, :, None] * values
        )
        gated_rows = readout.reshape(row_count, head_count * head_width) * jax.nn.silu(
            gate_tokens[step_index].astype(jnp.float32)
        )
        grouped = gated_rows.reshape(row_count, group_count, group_span)
        factor = lax.rsqrt(jnp.mean(grouped * grouped, axis=-1, keepdims=True) + 1e-05)
        normed = (grouped * factor).reshape(row_count, head_count * head_width) * norm_gain.astype(
            jnp.float32
        )
        normed_list.append(normed.astype(jnp.bfloat16))
    return (jnp.stack(normed_list), states_now)


def arrival_rows(received_ids, slot_count):
    wanted = jnp.arange(slot_count, dtype=jnp.int32)[:, None] == received_ids[None, :]
    buffer_index = jnp.arange(received_ids.shape[0], dtype=jnp.int32)
    return jnp.sum(jnp.where(wanted, buffer_index[None, :], 0), axis=1)


def shards(
    ssm_state,
    conv_state,
    dst_replica,
    dst_slot,
    live,
    conv_in,
    gate_in,
    dt_in,
    conv_weight,
    conv_bias,
    dt_bias,
    a_log,
    skip_gain,
    norm_gain,
    out_weight,
):
    replicas = lax.axis_size("replica")
    own_replica = lax.axis_index("replica")
    slot_count = ssm_state.shape[0]
    capacity = max(2, 2 * slot_count // replicas)
    row_index = jnp.arange(slot_count, dtype=jnp.int32)
    same_target = dst_replica[:, None] == dst_replica[None, :]
    earlier_rows = row_index[None, :] < row_index[:, None]
    member = jnp.sum(jnp.where(same_target & earlier_rows, 1, 0), axis=1).astype(jnp.int32)
    position = dst_replica * capacity + member
    buffer_rows = jnp.arange(replicas * capacity, dtype=jnp.int32)
    hit_table = position[None, :] == buffer_rows[:, None]
    picked = jnp.sum(jnp.where(hit_table, row_index[None, :], 0), axis=1)
    filled = jnp.any(hit_table, axis=1)
    send_ids = jnp.where(filled, jnp.take(dst_slot, picked), -1)
    send_windows = jnp.where(
        filled[:, None, None, None],
        jnp.take(conv_state, picked, axis=0),
        jnp.zeros((), conv_state.dtype),
    )
    send_states = jnp.where(
        filled[:, None, None, None],
        jnp.take(ssm_state, picked, axis=0),
        jnp.zeros((), ssm_state.dtype),
    )
    got_states, got_windows, got_ids = (
        lax.all_to_all(send_states, "replica", split_axis=0, concat_axis=0, tiled=True),
        lax.all_to_all(send_windows, "replica", split_axis=0, concat_axis=0, tiled=True),
        lax.all_to_all(send_ids, "replica", split_axis=0, concat_axis=0, tiled=True),
    )
    arrival = arrival_rows(got_ids, slot_count)
    windows_now = jnp.take(got_windows, arrival, axis=0)
    activations, windows_end = convolve(windows_now, conv_in, conv_weight, conv_bias)
    states_now = jnp.take(got_states, arrival, axis=0).astype(jnp.float32)
    normed_all, states_end = advance(
        states_now,
        activations,
        dt_in,
        gate_in,
        dt_bias,
        a_log,
        skip_gain,
        norm_gain,
        HEADS // GROUPS,
    )
    step_count = normed_all.shape[0]
    partial_value = jnp.dot(
        normed_all.reshape(step_count * slot_count, normed_all.shape[2]),
        out_weight,
        preferred_element_type=jnp.float32,
    )
    summed = lax.psum(partial_value, "tensor").astype(jnp.bfloat16)
    live_rows = row_index < live[own_replica]
    mixed = jnp.where(
        live_rows[None, :, None],
        summed.reshape(step_count, slot_count, summed.shape[1]),
        jnp.zeros((), jnp.bfloat16),
    )
    ssm_after = jnp.where(
        live_rows[:, None, None, None], states_end.astype(jnp.bfloat16), jnp.zeros((), jnp.bfloat16)
    )
    conv_after = jnp.where(
        live_rows[:, None, None, None], windows_end, jnp.zeros((), windows_end.dtype)
    )
    return (mixed, ssm_after, conv_after)


def solution(mesh):
    placed = (
        P(("groups", "replica"), "tensor", None, None),
        P(("groups", "replica"), None, "tensor", None),
        P(("groups", "replica")),
        P(("groups", "replica")),
        P("groups"),
        P(None, ("groups", "replica"), "tensor", None),
        P(None, ("groups", "replica"), "tensor"),
        P(None, ("groups", "replica"), "tensor"),
        P(None, "tensor", None),
        P("tensor", None),
        P("tensor"),
        P("tensor"),
        P("tensor"),
        P("tensor"),
        P("tensor", None),
    )
    return jax.shard_map(
        shards,
        mesh=mesh,
        in_specs=placed,
        out_specs=(
            P(None, ("groups", "replica"), None),
            P(("groups", "replica"), "tensor", None, None),
            P(("groups", "replica"), None, "tensor", None),
        ),
        check_vma=False,
    )
```

profile of v0, /device:TPU:5, one launch (start us, length us, event | category | flops | bytes accessed | tf_op | source)
XLA Modules:
  0.0 168.5 jit_solution(12787749655100111528)
XLA Ops:
  0.6 1.0 select_reduce_fusion.2
  1.6 0.7 multiply_add_fusion.6
  2.6 1.3 gather_fusion
  4.1 0.6 select_select_fusion.1
  4.7 4.6 %all-to-all-start = ((s32[4,4,1]{1,2,0:T(1,128)}), s32[4,4,1]{1,2,0:T(1,128)S(1)}, u32[]{:S(2)}, u32[]{:S(2)}) async-start(s32[4,4,1]{1,2,0:T(1,128)} %bitcast.4), calls=%async_computation | async-start | bytes 4096 | tf_op jit(solution)/shard_map/all_to_all | solution.py:117
  9.3 0.9 copy.46
  10.1 0.7 gather_fusion.3
  10.8 0.9 fusion.14
  11.7 3.1 %gather_fusion.1 = bf16[16,16,64,128]{3,2,1,0:T(8,128)(2,1)} fusion(bf16[8,16,64,128]{3,2,1,0:T(8,128)(2,1)S(1)} %copy-done, s32[1024]{0:T(1024)S(1)} %pad_clamp_fusion.1), kind=kCustom, calls=%fused_computation.1 | custom fusion | bytes 8388672 | tf_op jit(solution)/shard_map/jit(_take)/gather | solution.py:111
  14.8 4.5 %all-to-all-start.2 = ((bf16[16,3,1,1280]{3,1,2,0:T(4,128)(2,1)}), bf16[16,3,1,1280]{3,1,2,0:T(4,128)(2,1)S(1)}, u32[]{:S(2)}, u32[]{:S(2)}) async-start(bf16[16,3,1,1280]{3,1,2,0:T(4,128)(2,1)} %fusion.14), calls=%async_computation.2 | async-start | bytes 327680 | tf_op jit(solution)/shard_map/all_to_all | solution.py:116
  19.3 4.7 %select_select_fusion = bf16[16,16,64,128]{3,2,1,0:T(8,128)(2,1)} fusion(bf16[16,16,64,128]{3,2,1,0:T(8,128)(2,1)} %gather_fusion.1, pred[16]{0:T(512)(128)(4,1)S(1)} %compare_and_fusion, pred[16]{0:T(512)(128)(4,1)S(1)} %fusion.31), kind=kLoop, calls=%fused_computation.8 | loop fusion | flops 4194304 | bytes 8388640 | tf_op jit(solution)/shard_map/jit(_where)/select_n | solution.py:109
  24.2 4.9 %all-to-all-start.1 = ((bf16[16,16,64,128]{3,2,1,0:T(8,128)(2,1)}), bf16[16,16,64,128]{3,2,1,0:T(8,128)(2,1)}, u32[]{:S(2)}, u32[]{:S(2)}) async-start(bf16[16,16,64,128]{3,2,1,0:T(8,128)(2,1)} %select_select_fusion), calls=%async_computation.1 | async-start | bytes 8388608 | tf_op jit(solution)/shard_map/all_to_all | solution.py:115
  29.9 0.6 iota_compare_fusion.3
  31.2 0.7 reduce.9
  32.1 0.6 gather_fusion.4
  33.7 0.6 copy.40
  34.5 87.3 %all-to-all-done.1 = bf16[16,16,64,128]{3,2,1,0:T(8,128)(2,1)} async-done(((bf16[16,16,64,128]{3,2,1,0:T(8,128)(2,1)}), bf16[16,16,64,128]{3,2,1,0:T(8,128)(2,1)}, u32[]{:S(2)}, u32[]{:S(2)}) %all-to-all-start.1) | async-done | bytes 4194336 | tf_op jit(solution)/shard_map/all_to_all | solution.py:115
  121.8 4.3 %gather_fusion.2 = bf16[8,16,64,128]{3,2,1,0:T(8,128)(2,1)} fusion(bf16[16,16,64,128]{3,2,1,0:T(8,128)(2,1)} %all-to-all-done.1, s32[1024]{0:T(1024)S(1)} %pad_clamp_fusion), kind=kCustom, calls=%fused_computation.2 | custom fusion | bytes 4194336 | tf_op jit(solution)/shard_map/jit(_take)/gather | solution.py:122
  126.1 5.5 %fusion.3 = bf16[8,16,64,128]{3,2,1,0:T(8,128)(2,1)} fusion(f32[8,128]{1,0:T(8,128)S(1)} %get-tuple-element.24, f32[8,16,64]{2,1,0:T(8,128)S(1)} %get-tuple-element.42, f32[8,16]{1,0:T(8,128)S(1)} %get-tuple-element.35, f32[8,128]{1,0:T(8,128)S(1)} %get-tuple-element.40, f32[8,16,64]{2,1,0:T(8,128)S(1)} %get-tuple-element.43, ...), kind=kLoop, calls=%fused_computation.11 | loop fusion | flops 10485760 | bytes 4269072 | tf_op jit(solution)/shard_map/jit(_where)/select_n | solution.py:147
  131.6 9.4 %fusion.2 = f32[8,16,1,64]{3,2,1,0:T(1,128)S(1)} fusion(f32[8,16,128,1]{2,3,1,0:T(1,128)S(1)} %bitcast.83, f32[8,128]{1,0:T(8,128)S(1)} %get-tuple-element.24, f32[8,16,64]{2,1,0:T(8,128)S(1)} %get-tuple-element.42, f32[8,16]{1,0:T(8,128)S(1)} %get-tuple-element.35, f32[8,128]{1,0:T(8,128)S(1)} %get-tuple-element.40, ...), kind=kOutput, calls=%fused_computation.10 | convolution fusion | flops 20971520 | bytes 2270216 | tf_op jit(solution)/shard_map/shpn,shn->shp/dot_general | solution.py:52
  141.1 7.1 %fusion = f32[8,16,1,64]{3,2,1,0:T(1,128)S(1)} fusion(f32[8,16,128,1]{2,3,1,0:T(1,128)S(1)} %bitcast.82, f32[8,128]{1,0:T(8,128)S(1)} %get-tuple-element.40, f32[8,16,64]{2,1,0:T(8,128)S(1)} %get-tuple-element.43, f32[8,16]{1,0:T(8,128)S(1)} %get-tuple-element.34, bf16[8,16,64,128]{3,2,1,0:T(8,128)(2,1)S(1)} %copy-done.1, pred[8]{0:T(512)(128)(4,1)S(1)} %compare_and_fusion.1), kind=kOutput, calls=%fused_computation.7 | convolution fusion | flops 17825792 | bytes 2232840 | tf_op jit(solution)/shard_map/shpn,shn->shp/dot_general | solution.py:52
  148.6 4.6 %fusion.16 = f32[16,4096]{1,0:T(8,128)S(1)} fusion(bf16[1024,4096]{1,0:T(8,128)(2,1)} %param.29, bf16[1,8,1024]{2,1,0:T(8,128)(2,1)S(1)} %get-tuple-element.29, bf16[1,8,1024]{2,1,0:T(8,128)(2,1)S(1)} %get-tuple-element.28), kind=kOutput, calls=%fused_computation.43 | convolution fusion | flops 134234112 | bytes 8683520 | tf_op jit(solution)/shard_map/dot_general | solution.py:135
  153.2 14.5 %all-reduce.1 = bf16[16,4096]{1,0:T(8,128)(2,1)S(1)} all-reduce(f32[16,4096]{1,0:T(8,128)S(1)} %fusion.16), channel_id=1, replica_groups=mesh['groups'=2,'replica'=4,'tensor'=4] {'tensor'}, use_global_device_ids=true, to_apply=%region_8.9 | all-reduce | flops 65536 | bytes 393216 | tf_op jit(solution)/shard_map/psum | solution.py:140
  167.8 0.7 bitcast_select_fusion.1
  (71 shorter events, 3.8 us)
Async XLA Ops:
  0.6 11.1 %copy-start = (bf16[8,16,64,128]{3,2,1,0:T(8,128)(2,1)S(1)}, bf16[8,16,64,128]{3,2,1,0:T(8,128)(2,1)}, u32[]{:S(2)}) copy-start(bf16[8,16,64,128]{3,2,1,0:T(8,128)(2,1)} %param.15) | copy-start | bytes 6291460
  4.7 10.1 %all-to-all-start = ((s32[4,4,1]{1,2,0:T(1,128)}), s32[4,4,1]{1,2,0:T(1,128)S(1)}, u32[]{:S(2)}, u32[]{:S(2)}) async-start(s32[4,4,1]{1,2,0:T(1,128)} %bitcast.4), calls=%async_computation | async-start | bytes 4096 | tf_op jit(solution)/shard_map/all_to_all | solution.py:117
  14.8 9.4 %all-to-all-start.2 = ((bf16[16,3,1,1280]{3,1,2,0:T(4,128)(2,1)}), bf16[16,3,1,1280]{3,1,2,0:T(4,128)(2,1)S(1)}, u32[]{:S(2)}, u32[]{:S(2)}) async-start(bf16[16,3,1,1280]{3,1,2,0:T(4,128)(2,1)} %fusion.14), calls=%async_computation.2 | async-start | bytes 327680 | tf_op jit(solution)/shard_map/all_to_all | solution.py:116
  24.0 5.1 %copy-start.3 = (bf16[2,8,1,1280]{3,1,2,0:T(8,128)(2,1)S(1)}, bf16[2,8,1,1280]{3,1,2,0:T(8,128)(2,1)}, u32[]{:S(2)}) copy-start(bf16[2,8,1,1280]{3,1,2,0:T(8,128)(2,1)} %param.20) | copy-start | bytes 122884
  24.0 5.2 %copy-start.2 = (bf16[2,8,1024]{2,1,0:T(8,128)(2,1)S(1)}, bf16[2,8,1024]{2,1,0:T(8,128)(2,1)}, u32[]{:S(2)}) copy-start(bf16[2,8,1024]{2,1,0:T(8,128)(2,1)} %param.21) | copy-start | bytes 98308
  24.0 5.4 %copy-start.7 = (bf16[1024]{0:T(1024)(128)(2,1)S(1)}, bf16[1024]{0:T(1024)(128)(2,1)}, u32[]{:S(2)}) copy-start(bf16[1024]{0:T(1024)(128)(2,1)} %param.28) | copy-start | bytes 6148
  24.0 5.4 %copy-start.10 = (s32[4]{0:T(128)S(1)}, s32[4]{0:T(128)}, u32[]{:S(2)}) copy-start(s32[4]{0:T(128)} %param.19) | copy-start | bytes 52
  24.0 6.6 %copy-start.5 = (bf16[1,1280]{1,0:T(2,128)(2,1)S(1)}, bf16[1,1280]{1,0:T(2,128)(2,1)}, u32[]{:S(2)}) copy-start(bf16[1,1280]{1,0:T(2,128)(2,1)} %param.24) | copy-start | bytes 7684
  24.0 6.6 %copy-start.11 = (f32[16]{0:T(128)S(1)}, f32[16]{0:T(128)}, u32[]{:S(2)}) copy-start(f32[16]{0:T(128)} %param.26) | copy-start | bytes 196
  24.0 6.6 %copy-start.6 = (bf16[2,8,16]{2,1,0:T(8,128)(2,1)S(1)}, bf16[2,8,16]{2,1,0:T(8,128)(2,1)}, u32[]{:S(2)}) copy-start(bf16[2,8,16]{2,1,0:T(8,128)(2,1)} %param.22) | copy-start | bytes 1540
  24.0 6.6 %copy-start.9 = (f32[16]{0:T(128)S(1)}, f32[16]{0:T(128)}, u32[]{:S(2)}) copy-start(f32[16]{0:T(128)} %param.25) | copy-start | bytes 196
  24.0 6.7 %copy-start.4 = (bf16[4,1,1280]{2,0,1:T(4,128)(2,1)S(1)}, bf16[4,1,1280]{2,0,1:T(4,128)(2,1)}, u32[]{:S(2)}) copy-start(bf16[4,1,1280]{2,0,1:T(4,128)(2,1)} %param.23) | copy-start | bytes 30724
  24.2 97.6 %all-to-all-start.1 = ((bf16[16,16,64,128]{3,2,1,0:T(8,128)(2,1)}), bf16[16,16,64,128]{3,2,1,0:T(8,128)(2,1)}, u32[]{:S(2)}, u32[]{:S(2)}) async-start(bf16[16,16,64,128]{3,2,1,0:T(8,128)(2,1)} %select_select_fusion), calls=%async_computation.1 | async-start | bytes 8388608 | tf_op jit(solution)/shard_map/all_to_all | solution.py:115
  126.1 5.5 %copy-start.1 = (bf16[8,16,64,128]{3,2,1,0:T(8,128)(2,1)S(1)}, bf16[8,16,64,128]{3,2,1,0:T(8,128)(2,1)}, u32[]{:S(2)}) copy-start(bf16[8,16,64,128]{3,2,1,0:T(8,128)(2,1)} %gather_fusion.2) | copy-start | bytes 6291460
  141.0 7.1 %copy-start.8 = (f32[16]{0:T(128)S(1)}, f32[16]{0:T(128)}, u32[]{:S(2)}) copy-start(f32[16]{0:T(128)} %param.27) | copy-start | bytes 196
where the time goes:
time: 170 us; the launch traced here: 169 us
  waiting for transfers between devices  87.4 us (51%)
  matrix products  21.1 us (12%)
  other arithmetic  17 us (10%)
  blocking collectives  14.5 us (9%)
  starting transfers between devices  14 us (8%)
  local copies, waits for them, and re-layouts  13.6 us (8%)
    all_to_all x1, waiting for transfers between devices, shards(): lax.all_to_all(send_states, 'replica', split_axis=0, concat_axis=0, tiled...  87.3 us
    dot_general x2, matrix products, advance(): jnp.einsum('shpn,shn->shp', states_now, output_map, precision=lax.Precisi...  16.5 us
    psum x1, blocking collectives, shards(): summed = lax.psum(partial_value, 'tensor').astype(jnp.bfloat16)  14.5 us
    select_n x1, other arithmetic, shards(): jnp.where(live_rows[:, None, None, None], states_end.astype(jnp.bfloat16)...  5.49 us
    all_to_all x1, starting transfers between devices, shards(): lax.all_to_all(send_states, 'replica', split_axis=0, concat_axis=0, tiled...  4.86 us
    select_n x1, other arithmetic, shards(): jnp.where(filled[:, None, None, None], jnp.take(ssm_state, picked, axis=0...  4.69 us
    all_to_all x1, starting transfers between devices, shards(): lax.all_to_all(send_ids, 'replica', split_axis=0, concat_axis=0, tiled=True)  4.59 us
    dot_general x1, matrix products, shards(): jnp.dot(normed_all.reshape(step_count * slot_count, normed_all.shape[2]),...  4.59 us
  transfers between devices with their start and end apart: 3, of which 2 were waited for; matrix products, arithmetic and copies ran while one was open for 9% of the time, Pallas kernels for 0%

commit v1 on v0

--- a/solution.py
+++ b/solution.py
@@ -1,10 +1,520 @@
+import functools
+import itertools
+
 import jax
 import jax.numpy as jnp
 from jax import lax
+from jax.experimental import pallas as pl
+from jax.experimental.pallas import tpu as pltpu
 from jax.sharding import PartitionSpec as P
 
 HEADS = 64
 GROUPS = 4
+BF16 = jnp.bfloat16
+F32 = jnp.float32
+SMEM = pltpu.SMEM
+VMEM = pltpu.VMEM
+
+
+def send_graphs(replicas):
+    pairs = list(itertools.combinations(range(replicas), 2))
+    graphs = []
+    for chosen in itertools.product(pairs, repeat=replicas):
+        if any(sum(d in pair for pair in chosen) != 2 for d in range(replicas)):
+            continue
+        for picks in itertools.product((0, 1), repeat=replicas):
+            first = [chosen[s][picks[s]] for s in range(replicas)]
+            if len(set(first)) == replicas:
+                second = [chosen[s][1 - picks[s]] for s in range(replicas)]
+                break
+        code = sum(1 << (replicas * s + d) for s in range(replicas) for d in chosen[s])
+        bits = sum(picks[s] << s for s in range(replicas))
+        graphs.append((code, bits, first, second))
+    return graphs
+
+
+def route_kernel(graphs, replicas, slots, *refs):
+    metas = refs[:replicas]
+    states, windows, buf_a, buf_b, branch, arrival, win_rows, sems = refs[replicas:]
+    half = slots // 2
+    span = states.shape[1]
+    taps = windows.shape[0]
+    lanes = states.shape[2]
+    block = win_rows.shape[1]
+    me = lax.axis_index("replica")
+    sources = [lax.rem(me + (replicas - k), replicas) for k in range(replicas)]
+    code = jnp.int32(0)
+    for k in range(replicas):
+        edges = jnp.int32(0)
+        for i in range(slots):
+            edges = edges + jnp.left_shift(jnp.int32(1), metas[k][i])
+        code = code + jnp.left_shift(lax.div(edges, jnp.int32(half)), sources[k] * replicas)
+    index = jnp.int32(0)
+    bits = jnp.int32(0)
+    for j, (graph_code, graph_bits, _, _) in enumerate(graphs):
+        hit = code == graph_code
+        index = jnp.where(hit, j, index)
+        bits = jnp.where(hit, graph_bits, bits)
+    branch[0] = index
+
+    def second_matching(source, target):
+        row = lax.bitwise_and(
+            lax.shift_right_logical(code, source * replicas), jnp.int32((1 << replicas) - 1)
+        )
+        below = lax.bitwise_and(row, jnp.left_shift(jnp.int32(1), target) - 1)
+        rank = jnp.where(below != 0, 1, 0)
+        pick = lax.bitwise_and(lax.shift_right_logical(bits, source), jnp.int32(1))
+        return jnp.where(rank == pick, 0, 1)
+
+    def pack(buf, place, i):
+        rows = pl.ds(pl.multiple_of(place * span, span), span)
+        return pltpu.make_async_copy(states.at[i], buf.at[rows], sems.at[i])
+
+    counts = [jnp.int32(0), jnp.int32(0)]
+    picked = []
+    for i in range(slots):
+        which = second_matching(me, metas[0][i])
+        place = jnp.where(which == 0, counts[0], counts[1])
+        counts = [counts[0] + (1 - which), counts[1] + which]
+        picked.append((which, place))
+        for m, buf in enumerate((buf_a, buf_b)):
+
+            @pl.when(which == m)
+            def _(buf=buf, i=i, place=place):
+                pack(buf, place, i).start()
+
+    for k in range(replicas):
+        which = second_matching(sources[k], me)
+        base = which * half + (2 * half if k == 0 else 0)
+        count = jnp.int32(0)
+        for i in range(slots):
+            mine = metas[k][i] == me
+
+            @pl.when(mine)
+            def _(k=k, i=i, base=base, count=count):
+                arrival[metas[k][slots + i]] = base + count
+
+            count = count + jnp.where(mine, 1, 0)
+
+    win_rows[...] = jnp.zeros_like(win_rows)
+    for tap in range(taps):
+        tokens = windows[tap].astype(F32)
+        for i in range(slots):
+            which, place = picked[i]
+            win_rows[which, pl.ds(tap * half + place, 1), :] = tokens[i : i + 1]
+    for m, buf in enumerate((buf_a, buf_b)):
+        rows = win_rows[m].astype(BF16)
+        for part in range(rows.shape[1] // lanes):
+            top = half * span + part * block
+            buf[top : top + block, :] = rows[:, part * lanes : (part + 1) * lanes]
+
+    for i in range(slots):
+        which, place = picked[i]
+        for m, buf in enumerate((buf_a, buf_b)):
+
+            @pl.when(which == m)
+            def _(buf=buf, i=i, place=place):
+                pack(buf, place, i).wait()
+
+
+def parts_of(value, count):
+    out = []
+    for _ in range(count):
+        part = value.astype(BF16).astype(F32)
+        out.append(part)
+        value = value - part
+    return out
+
+
+def sum_of_parts(rows, count):
+    size = rows.shape[0] // count
+    total = rows[:size]
+    for part in range(1, count):
+        total = total + rows[part * size : (part + 1) * size]
+    return total
+
+
+def silu(value):
+    return value / (1.0 + jnp.exp(-value))
+
+
+def softplus(value):
+    return jnp.maximum(value, 0.0) + jnp.log1p(jnp.exp(-jnp.abs(value)))
+
+
+def row_copy(arrival, sources, held, sems, row, act):
+    slots, span, _ = held.shape
+    half = slots // 2
+    place = arrival[row]
+    which = lax.div(place, half)
+    rows = pl.ds(pl.multiple_of(lax.rem(place, half) * span, span), span)
+    for m, source in enumerate(sources):
+
+        @pl.when(which == m)
+        def _(source=source):
+            act(pltpu.make_async_copy(source.at[rows], held.at[row], sems.at[row]))
+
+
+def mix_kernel(
+    arrival,
+    live,
+    got_a,
+    got_b,
+    own_a,
+    own_b,
+    conv_in,
+    gate_in,
+    dt_in,
+    conv_weight,
+    conv_bias,
+    dt_bias,
+    a_log,
+    skip_gain,
+    norm_gain,
+    out_weight,
+    partial,
+    updates,
+    inputs,
+    scale,
+    last_window,
+    held,
+    weight_held,
+    win_held,
+    win_all,
+    win_rows,
+    in_sem,
+    win_sem,
+    weight_sem,
+):
+    slots, span, state = held.shape
+    heads = dt_in.shape[2]
+    half = slots // 2
+    taps = win_rows.shape[0]
+    chunk = out_weight.shape[0] // weight_sem.shape[0]
+    sources = (got_a, got_b, own_a, own_b)
+    win_size = win_held.shape[1]
+    block = win_all.shape[1]
+
+    def win_copy(m):
+        return pltpu.make_async_copy(
+            sources[m].at[pl.ds(half * span, win_size)], win_held.at[m], win_sem.at[m]
+        )
+
+    def weight_copy(part):
+        rows = pl.ds(part * chunk, chunk)
+        return pltpu.make_async_copy(
+            out_weight.at[rows], weight_held.at[rows], weight_sem.at[part]
+        )
+
+    for m in range(len(sources)):
+        win_copy(m).start()
+    for row in range(slots):
+        row_copy(arrival, sources, held, in_sem, row, lambda copy: copy.start())
+    for part in range(weight_sem.shape[0]):
+        weight_copy(part).start()
+
+    steps, kept = [], []
+    for step in range(2):
+        steps.append(softplus(dt_in[step].astype(F32) + dt_bias[...]))
+        kept.append(jnp.exp(steps[step] * -jnp.exp(a_log[...])))
+    scale[...] = kept[0] * kept[1]
+    per_head = jnp.concatenate(
+        steps + kept + [jnp.broadcast_to(skip_gain[...], (slots, heads))], axis=0
+    )
+    head_of = lax.div(lax.broadcasted_iota(jnp.int32, (heads, span), 1), span // heads)
+    spread = jnp.where(
+        head_of == lax.broadcasted_iota(jnp.int32, (heads, span), 0), 1.0, 0.0
+    ).astype(BF16)
+    wide = sum_of_parts(
+        jnp.dot(
+            jnp.concatenate(parts_of(per_head, 3), axis=0).astype(BF16),
+            spread,
+            preferred_element_type=F32,
+        ),
+        3,
+    )
+    step_size = [wide[:slots], wide[slots : 2 * slots]]
+    retained = [wide[2 * slots : 3 * slots], wide[3 * slots : 4 * slots]]
+    skip = wide[4 * slots :]
+
+    for m in range(len(sources)):
+        win_copy(m).wait()
+        for part in range(win_size // block):
+            win_all[m, :, part * state : (part + 1) * state] = win_held[
+                m, part * block : (part + 1) * block, :
+            ].astype(F32)
+    for row in range(slots):
+        place = arrival[row]
+        which = lax.div(place, half)
+        member = lax.rem(place, half)
+        for tap in range(taps):
+            win_rows[tap, row : row + 1, :] = win_all[
+                which, pl.ds(tap * half + member, 1), :
+            ]
+    last_window[...] = win_rows[taps - 1]
+
+    line = [win_rows[tap] for tap in range(taps)] + [
+        conv_in[0].astype(F32),
+        conv_in[1].astype(F32),
+    ]
+    weights = conv_weight[...].astype(F32)
+    acts = []
+    for step in range(2):
+        total = line[step] * weights[0:1]
+        for tap in range(1, taps + 1):
+            total = total + line[step + tap] * weights[tap : tap + 1]
+        acts.append(silu(total + conv_bias[...].astype(F32)))
+    xs = [act[:, :span] for act in acts]
+    bs = [act[:, span : span + state] for act in acts]
+    cs = [act[:, span + state :] for act in acts]
+    us = [step_size[0] * xs[0], step_size[1] * xs[1]]
+    updates[0] = retained[1] * us[0]
+    updates[1] = us[1]
+    inputs[0] = bs[0]
+    inputs[1] = bs[1]
+    queries = jnp.concatenate(parts_of(jnp.concatenate(cs, axis=0), 3), axis=0).astype(BF16)
+    row_of = lax.rem(lax.broadcasted_iota(jnp.int32, (2 * slots, span), 0), slots)
+
+    ys = jnp.zeros((2 * slots, span), F32)
+    for row in range(slots):
+        row_copy(arrival, sources, held, in_sem, row, lambda copy: copy.wait())
+        got = lax.dot_general(
+            queries, held[row], (((1,), (1,)), ((), ())), preferred_element_type=F32
+        )
+        ys = jnp.where(row_of == row, sum_of_parts(got, 3), ys)
+
+    def dots(b, c):
+        return jnp.sum(b * c, axis=1, keepdims=True)
+
+    reads = [
+        retained[0] * ys[:slots] + us[0] * dots(bs[0], cs[0]) + skip * xs[0],
+        retained[1] * (retained[0] * ys[slots:] + us[0] * dots(bs[0], cs[1]))
+        + us[1] * dots(bs[1], cs[1])
+        + skip * xs[1],
+    ]
+    gains = norm_gain[...].astype(F32)
+    normed = []
+    for step in range(2):
+        gated = reads[step] * silu(gate_in[step].astype(F32))
+        factor = lax.rsqrt(jnp.sum(gated * gated, axis=1, keepdims=True) * (1.0 / span) + 1e-05)
+        normed.append((gated * factor) * gains)
+    normed = jnp.concatenate(normed, axis=0)
+    alive = live[lax.axis_index("replica")]
+    normed = jnp.where(row_of < alive, normed, 0.0).astype(BF16)
+    total = None
+    for part in range(weight_sem.shape[0]):
+        weight_copy(part).wait()
+        cut = slice(part * chunk, (part + 1) * chunk)
+        term = jnp.dot(normed[:, cut], weight_held[cut, :], preferred_element_type=F32)
+        total = term if total is None else total + term
+    partial[...] = total.astype(BF16)
+
+
+def state_kernel(
+    arrival,
+    live,
+    got_a,
+    got_b,
+    own_a,
+    own_b,
+    updates,
+    inputs,
+    scale,
+    last_window,
+    conv_in,
+    states_out,
+    windows_out,
+    held,
+    held_out,
+    in_sem,
+    out_sem,
+):
+    slots, span, state = held.shape
+    heads = scale.shape[1]
+    width = span // heads
+    sources = (got_a, got_b, own_a, own_b)
+    for row in range(slots):
+        row_copy(arrival, sources, held, in_sem, row, lambda copy: copy.start())
+    alive = live[lax.axis_index("replica")]
+    keep = lax.broadcasted_iota(jnp.int32, last_window.shape, 0) < alive
+    for tap, tokens in enumerate(
+        (last_window[...], conv_in[0].astype(F32), conv_in[1].astype(F32))
+    ):
+        windows_out[tap] = jnp.where(keep, tokens, 0.0).astype(BF16)
+
+    u_parts, b_parts = [], []
+    for step in range(2):
+        u_hi, u_lo = parts_of(updates[step], 2)
+        b_hi, b_lo = parts_of(inputs[step], 2)
+        u_parts += [u_hi, u_hi, u_lo, u_lo]
+        b_parts += [b_hi, b_lo, b_hi, b_lo]
+    u_columns = jnp.transpose(jnp.concatenate(u_parts, axis=0)).astype(BF16)
+    b_rows = jnp.concatenate(b_parts, axis=0)
+    b_of = lax.rem(lax.broadcasted_iota(jnp.int32, b_rows.shape, 0), slots)
+    for row in range(slots):
+        row_copy(arrival, sources, held, in_sem, row, lambda copy: copy.wait())
+        added = jnp.dot(
+            u_columns,
+            jnp.where(b_of == row, b_rows, 0.0).astype(BF16),
+            preferred_element_type=F32,
+        )
+        for head in range(heads):
+            rows = slice(head * width, (head + 1) * width)
+            value = (
+                scale[row : row + 1, head : head + 1] * held[row, rows, :].astype(F32)
+                + added[rows]
+            )
+            held_out[row, rows, :] = jnp.where(row < alive, value, 0.0).astype(BF16)
+        pltpu.make_async_copy(held_out.at[row], states_out.at[row], out_sem.at[row]).start()
+    for row in range(slots):
+        pltpu.make_async_copy(held_out.at[row], states_out.at[row], out_sem.at[row]).wait()
+
+
+def routed(
+    ssm_state,
+    conv_state,
+    dst_replica,
+    dst_slot,
+    live,
+    conv_in,
+    gate_in,
+    dt_in,
+    conv_weight,
+    conv_bias,
+    dt_bias,
+    a_log,
+    skip_gain,
+    norm_gain,
+    out_weight,
+):
+    replicas = lax.axis_size("replica")
+    slots, heads, width, state = ssm_state.shape
+    half = slots // 2
+    span = heads * width
+    taps, channels = conv_state.shape[1], conv_state.shape[3]
+    columns = out_weight.shape[1]
+    graphs = send_graphs(replicas)
+    block = 16 * pl.cdiv(half * taps, 16)
+    win_size = block * (channels // state)
+
+    meta = jnp.concatenate([dst_replica, dst_slot])
+    metas = [meta] + [
+        lax.ppermute(meta, "replica", [(s, (s + k) % replicas) for s in range(replicas)])
+        for k in range(1, replicas)
+    ]
+    tokens = conv_in.reshape(2, slots, channels)
+
+    any_spec = pl.BlockSpec(memory_space=pl.ANY)
+    smem = pl.BlockSpec(memory_space=SMEM)
+    vmem = pl.BlockSpec(memory_space=VMEM)
+    packed = jax.ShapeDtypeStruct((half * span + win_size, state), BF16)
+    own_a, own_b, branch, arrival = pl.pallas_call(
+        functools.partial(route_kernel, graphs, replicas, slots),
+        out_shape=(
+            packed,
+            packed,
+            jax.ShapeDtypeStruct((1,), jnp.int32),
+            jax.ShapeDtypeStruct((slots,), jnp.int32),
+        ),
+        in_specs=[smem] * replicas + [any_spec, vmem],
+        out_specs=(vmem, vmem, smem, smem),
+        scratch_shapes=[VMEM((2, block, channels), F32), pltpu.SemaphoreType.DMA((slots,))],
+        name="route",
+    )(
+        *metas,
+        ssm_state.reshape(slots, span, state),
+        jnp.swapaxes(conv_state, 0, 1).reshape(taps, slots, channels),
+    )
+
+    def along(first, second):
+        def send(rows_a, rows_b):
+            out = []
+            for value, targets in ((rows_a, first), (rows_b, second)):
+                moves = [(s, d) for s, d in enumerate(targets) if s != d]
+                out.append(lax.ppermute(value, "replica", moves) if moves else value)
+            return tuple(out)
+
+        return send
+
+    got_a, got_b = lax.switch(
+        branch[0], [along(first, second) for _, _, first, second in graphs], own_a, own_b
+    )
+    arrived = (got_a, got_b, own_a, own_b)
+
+    weight_parts = 4
+    partial, updates, inputs, scale, last_window = pl.pallas_call(
+        mix_kernel,
+        out_shape=(
+            jax.ShapeDtypeStruct((2 * slots, columns), BF16),
+            jax.ShapeDtypeStruct((2, slots, span), F32),
+            jax.ShapeDtypeStruct((2, slots, state), F32),
+            jax.ShapeDtypeStruct((slots, heads), F32),
+            jax.ShapeDtypeStruct((slots, channels), F32),
+        ),
+        in_specs=[smem, smem] + [any_spec] * 4 + [vmem] * 9 + [any_spec],
+        out_specs=(vmem,) * 5,
+        scratch_shapes=[
+            VMEM((slots, span, state), BF16),
+            VMEM(out_weight.shape, BF16),
+            VMEM((4, win_size, state), BF16),
+            VMEM((4, block, channels), F32),
+            VMEM((taps, slots, channels), F32),
+            pltpu.SemaphoreType.DMA((slots,)),
+            pltpu.SemaphoreType.DMA((4,)),
+            pltpu.SemaphoreType.DMA((weight_parts,)),
+        ],
+        compiler_params=pltpu.CompilerParams(vmem_limit_bytes=52 * 2**20),
+        name="mix",
+    )(
+        arrival,
+        live,
+        *arrived,
+        tokens,
+        gate_in,
+        dt_in,
+        conv_weight.reshape(taps + 1, channels),
+        conv_bias,
+        dt_bias.reshape(1, heads),
+        a_log.reshape(1, heads),
+        skip_gain.reshape(1, heads),
+        norm_gain.reshape(1, span),
+        out_weight,
+    )
+
+    members = lax.axis_size("tensor")
+    terms = [partial] + [
+        lax.ppermute(partial, "tensor", [(i, i ^ k) for i in range(members)])
+        for k in range(1, members)
+    ]
+    states_out, windows_out = pl.pallas_call(
+        state_kernel,
+        out_shape=(
+            jax.ShapeDtypeStruct((slots, span, state), BF16),
+            jax.ShapeDtypeStruct((taps, slots, channels), BF16),
+        ),
+        in_specs=[smem, smem] + [any_spec] * 4 + [vmem] * 5,
+        out_specs=(any_spec, vmem),
+        scratch_shapes=[
+            VMEM((slots, span, state), BF16),
+            VMEM((slots, span, state), BF16),
+            pltpu.SemaphoreType.DMA((slots,)),
+            pltpu.SemaphoreType.DMA((slots,)),
+        ],
+        compiler_params=pltpu.CompilerParams(vmem_limit_bytes=32 * 2**20),
+        cost_estimate=pl.CostEstimate(
+            flops=40 * slots * span * state,
+            bytes_accessed=4 * slots * span * state,
+            transcendentals=0,
+        ),
+        name="states",
+    )(arrival, live, *arrived, updates, inputs, scale, last_window, tokens)
+
+    terms = [term.astype(F32) for term in terms]
+    while len(terms) > 1:
+        terms = [terms[i] + terms[i + 1] for i in range(0, len(terms), 2)]
+    mixed = terms[0].astype(BF16).reshape(2, slots, columns)
+    conv_after = jnp.swapaxes(windows_out, 0, 1)[:, :, None, :]
+    return mixed, states_out.reshape(ssm_state.shape), conv_after
 
 
 def convolve(window_rows, conv_tokens, conv_weight, conv_bias):
@@ -70,7 +580,7 @@
     return jnp.sum(jnp.where(wanted, buffer_index[None, :], 0), axis=1)
 
 
-def shards(
+def padded(
     ssm_state,
     conv_state,
     dst_replica,
@@ -171,6 +681,7 @@
         P("tensor"),
         P("tensor", None),
     )
+    shards = routed if mesh.shape["replica"] == 4 else padded
     return jax.shard_map(
         shards,
         mesh=mesh,

time: 170 us -> 101 us (0.59)
  matrix products: 21.1 us -> 0 us
  waiting for transfers between devices: 87.4 us -> 68.5 us
  other arithmetic: 17 us -> 1.47 us
  blocking collectives: 14.5 us -> 0 us
  Pallas kernels: 0 us -> 13.7 us
  local copies, waits for them, and re-layouts: 13.6 us -> 1.26 us
    all_to_all x3 -> x0, waiting for transfers between devices: 87.4 us -> none  [the longest x1 87.3 us: shards(): lax.all_to_all(send_states, 'replica', split_axis=0, concat_axis=0, tiled...]
    ppermute x0 -> x8, waiting for transfers between devices: none -> 68.5 us  [the longest x2 64.2 us: send(): out.append(lax.ppermute(value, 'replica', moves) if moves else value)]
    dot_general x3 -> x0, matrix products: 21.1 us -> none  [the longest x2 16.5 us: advance(): jnp.einsum('shpn,shn->shp', states_now, output_map, precision=lax.Precisi...]
    psum x1 -> x0, blocking collectives: 14.5 us -> none  [shards(): summed = lax.psum(partial_value, 'tensor').astype(jnp.bfloat16)]
    all_to_all x3 -> x0, starting transfers between devices: 14 us -> none  [the longest x1 4.86 us: shards(): lax.all_to_all(send_states, 'replica', split_axis=0, concat_axis=0, tiled...]
    pallas_call x0 -> x3, Pallas kernels: none -> 13.7 us  [the longest x1 5.34 us: routed(): pl.pallas_call(mix_kernel, out_shape=(jax.ShapeDtypeStruct((2 * slots, co...]
    ppermute x0 -> x8, starting transfers between devices: none -> 13.7 us  [the longest x2 5.21 us: send(): out.append(lax.ppermute(value, 'replica', moves) if moves else value)]
    select_n x9 -> x0, other arithmetic: 12.6 us -> none  [the longest x1 5.49 us: shards(): jnp.where(live_rows[:, None, None, None], states_end.astype(jnp.bfloat16)...]
  transfers between devices with their start and end apart: 3 -> 8, of which waited for: 2 -> 5; matrix products, arithmetic and copies ran while one was open for 9% -> 1% of each run, Pallas kernels for 0% -> 5%
where the time goes in v1:
time: 101 us; the launch traced here: 100 us
  waiting for transfers between devices  68.5 us (68%)
  starting transfers between devices  13.7 us (14%)
  Pallas kernels  13.7 us (14%)
  between operations  1.49 us (1%)
  other arithmetic  1.47 us (1%)
  local copies, waits for them, and re-layouts  1.26 us (1%)
    ppermute x2, waiting for transfers between devices, send(): out.append(lax.ppermute(value, 'replica', moves) if moves else value)  64.2 us
    pallas_call x1, Pallas kernels, routed(): pl.pallas_call(mix_kernel, out_shape=(jax.ShapeDtypeStruct((2 * slots, co...  5.34 us
    pallas_call x1, Pallas kernels, routed(): pl.pallas_call(state_kernel, out_shape=(jax.ShapeDtypeStruct((slots, span...  5.25 us
    ppermute x2, starting transfers between devices, send(): out.append(lax.ppermute(value, 'replica', moves) if moves else value)  5.21 us
    ppermute x3, starting transfers between devices, routed(): lax.ppermute(partial, 'tensor', [(i, i ^ k) for i in range(members)])  4.66 us
    ppermute x3, starting transfers between devices, routed(): lax.ppermute(meta, 'replica', [(s, (s + k) % replicas) for s in range(rep...  3.77 us
    pallas_call x1, Pallas kernels, routed(): pl.pallas_call(functools.partial(route_kernel, graphs, replicas, slots),...  3.08 us
    ppermute x3, waiting for transfers between devices, routed(): lax.ppermute(meta, 'replica', [(s, (s + k) % replicas) for s in range(rep...  3.04 us
  transfers between devices with their start and end apart: 8, of which 5 were waited for; matrix products, arithmetic and copies ran while one was open for 1% of the time, Pallas kernels for 5%

profile of v1, /device:TPU:5, one launch (start us, length us, event | category | flops | bytes accessed | tf_op | source)
XLA Modules:
  0.0 100.3 jit_solution(12345307501110172810)
XLA Ops:
  0.6 0.7 pad_add_fusion.refs_0_
  1.4 3.3 %collective-permute-start.173 = (s32[16]{0:T(128)S(1)}, s32[16]{0:T(128)S(1)}, u32[]{:S(2)}, u32[]{:S(2)}) collective-permute-start(s32[16]{0:T(128)S(1)} %pad_add_fusion.refs_0_), channel_id=1, source_target_pairs={{0,12},{4,0},{8,4},{12,8},{1,13},{5,1},{9,5},{13,9},{2,14},{6,2},{... | collective-permute-start | bytes 200 | tf_op jit(solution)/shard_map/ppermute | solution.py:402
  4.7 0.5 collective-permute-start.171
  5.2 0.7 reshape.46.norm_gain
  5.8 2.1 %collective-permute-done.172.refs_2_ = s32[16]{0:T(128)S(1)} collective-permute-done((s32[16]{0:T(128)S(1)}, s32[16]{0:T(128)S(1)}, u32[]{:S(2)}, u32[]{:S(2)}) %collective-permute-start.172) | collective-permute-done | bytes 96 | tf_op jit(solution)/shard_map/ppermute | solution.py:402
  8.0 0.9 collective-permute-done.171.refs_1_
  8.9 0.5 copy-done.13
  9.4 3.1 %route.1 = (bf16[4256,128]{1,0:T(8,128)(2,1)S(1)}, bf16[4256,128]{1,0:T(8,128)(2,1)S(1)}, s32[1]{0:T(128)}, s32[8]{0:T(128)}) custom-call(s32[16]{0:T(128)} %copy-done.10, s32[16]{0:T(128)} %copy-done.13, s32[16]{0:T(128)} %copy-done.12, s32[16]{0:T(128)} %copy-done.11, bf16[8,1024,128]{2,1,0:T(8,128)(2,1)} %bitcast.26, bf16[3,8,1280]{2,1,0:T(8,128)(2,1)} %bitcast.27), custom_call_target="tpu_custom_call" | custom-call | tf_op jit(solution)/shard_map/route/pallas_call | solution.py:411
  13.2 0.0 copy-start.2
  13.2 0.0 copy-start.3
  13.3 0.0 copy-start.7
  13.3 0.0 copy-start.8
  13.3 69.6 %conditional.1 = (bf16[4256,128]{1,0:T(8,128)(2,1)}, bf16[4256,128]{1,0:T(8,128)(2,1)}) conditional(s32[]{:T(128)} %bitcast.4, (bf16[4256,128]{1,0:T(8,128)(2,1)S(1)}, bf16[4256,128]{1,0:T(8,128)(2,1)S(1)}) %tuple.368, (bf16[4256,128]{1,0:T(8,128)(2,1)S(1)}, bf16[4256,128]{1,0:T(8,128)(2,1)S(1)}) %tuple.369, ...), branch_computations={%region_0.0_spmd, %region_1.0_spmd, %region_2.0_spmd, %region_3.0_... | conditional | bytes 8716384 | solution.py:439
  13.5 0.6 collective-permute-start.165
  14.2 4.6 %collective-permute-start.166 = (bf16[4256,128]{1,0:T(8,128)(2,1)S(1)}, bf16[4256,128]{1,0:T(8,128)(2,1)}, u32[]{:S(2)}, u32[]{:S(2)}) collective-permute-start(bf16[4256,128]{1,0:T(8,128)(2,1)S(1)} %get-tuple-element.535), channel_id=1, source_target_pairs={{0,12},{8,0},{12,8},{1,13},{9,1},{13,9},{2,14},{10,2},{14,10},{3,1... | collective-permute-start | bytes 3268616 | tf_op jit(solution)/shard_map/cond/branch_87_fun/ppermute | solution.py:434
  18.8 20.3 %collective-permute-done.165 = bf16[4256,128]{1,0:T(8,128)(2,1)} collective-permute-done((bf16[4256,128]{1,0:T(8,128)(2,1)S(1)}, bf16[4256,128]{1,0:T(8,128)(2,1)}, u32[]{:S(2)}, u32[]{:S(2)}) %collective-permute-start.165) | collective-permute-done | bytes 1089568 | tf_op jit(solution)/shard_map/cond/branch_87_fun/ppermute | solution.py:434
  39.0 43.9 %collective-permute-done.166 = bf16[4256,128]{1,0:T(8,128)(2,1)} collective-permute-done((bf16[4256,128]{1,0:T(8,128)(2,1)S(1)}, bf16[4256,128]{1,0:T(8,128)(2,1)}, u32[]{:S(2)}, u32[]{:S(2)}) %collective-permute-start.166) | collective-permute-done | bytes 1089568 | tf_op jit(solution)/shard_map/cond/branch_87_fun/ppermute | solution.py:434
  83.0 5.3 %mix.1 = (bf16[16,4096]{1,0:T(8,128)(2,1)S(1)}, f32[2,8,1024]{2,1,0:T(8,128)S(1)}, f32[2,8,128]{2,1,0:T(8,128)S(1)}, f32[8,16]{1,0:T(8,128)S(1)}, f32[8,1280]{1,0:T(8,128)S(1)}) custom-call(s32[8]{0:T(128)S(1)} %copy-done.6, s32[4]{0:T(128)S(1)} %copy-done.5, bf16[4256,128]{1,0:T(8,128)(2,1)} %get-tuple-element.560.got_a, ...), custom_call_target="tpu_custom_call" | custom-call | tf_op jit(solution)/shard_map/mix/pallas_call | solution.py:445
  88.4 4.2 %collective-permute-start.176 = (bf16[16,4096]{1,0:T(8,128)(2,1)S(1)}, bf16[16,4096]{1,0:T(8,128)(2,1)S(1)}, u32[]{:S(2)}, u32[]{:S(2)}) collective-permute-start(bf16[16,4096]{1,0:T(8,128)(2,1)S(1)} %get-tuple-element.562), channel_id=1, source_target_pairs={{0,3},{1,2},{2,1},{3,0},{4,7},{5,6},{6,5},{7,4},{8,11},{9,10},{10,... | collective-permute-start | bytes 393224 | tf_op jit(solution)/shard_map/ppermute | solution.py:486
  92.5 0.3 collective-permute-start.175
  92.8 0.2 collective-permute-start.174
  93.0 5.2 %states.1 = (bf16[8,1024,128]{2,1,0:T(8,128)(2,1)}, bf16[3,8,1280]{2,1,0:T(8,128)(2,1)}) custom-call(s32[8]{0:T(128)S(1)} %copy-done.6, s32[4]{0:T(128)S(1)} %copy-done.5, bf16[4256,128]{1,0:T(8,128)(2,1)} %get-tuple-element.560.got_a, bf16[4256,128]{1,0:T(8,128)(2,1)} %get-tuple-element.561.got_b, bf16[4256,128]{1,0:T(8,128)(2,1)S(1)} %get-tuple-element.559.own_a, ...), custom_call_target="tpu_custom_call" | custom-call | flops 41943040 | bytes 4194304 | tf_op jit(solution)/shard_map/states/pallas_call | solution.py:489
  98.3 1.3 %collective-permute-done.175 = bf16[16,4096]{1,0:T(8,128)(2,1)S(1)} collective-permute-done((bf16[16,4096]{1,0:T(8,128)(2,1)S(1)}, bf16[16,4096]{1,0:T(8,128)(2,1)S(1)}, u32[]{:S(2)}, u32[]{:S(2)}) %collective-permute-start.175) | collective-permute-done | bytes 131104 | tf_op jit(solution)/shard_map/ppermute | solution.py:486
  99.6 0.7 fusion
  (27 shorter events, 0.1 us)
Async XLA Ops:
  1.4 7.5 %copy-start.10 = (s32[16]{0:T(128)}, s32[16]{0:T(128)S(1)}, u32[]{:S(2)}) copy-start(s32[16]{0:T(128)S(1)} %pad_add_fusion.refs_0_) | copy-start | bytes 196
  1.4 4.5 %collective-permute-start.173 = (s32[16]{0:T(128)S(1)}, s32[16]{0:T(128)S(1)}, u32[]{:S(2)}, u32[]{:S(2)}) collective-permute-start(s32[16]{0:T(128)S(1)} %pad_add_fusion.refs_0_), channel_id=1, source_target_pairs={{0,12},{4,0},{8,4},{12,8},{1,13},{5,1},{9,5},{13,9},{2,14},{6,2},{... | collective-permute-start | bytes 200 | tf_op jit(solution)/shard_map/ppermute | solution.py:402
  4.7 3.3 %collective-permute-start.172 = (s32[16]{0:T(128)S(1)}, s32[16]{0:T(128)S(1)}, u32[]{:S(2)}, u32[]{:S(2)}) collective-permute-start(s32[16]{0:T(128)S(1)} %pad_add_fusion.refs_0_), channel_id=1, source_target_pairs={{0,8},{4,12},{8,0},{12,4},{1,9},{5,13},{9,1},{13,5},{2,10},{6,14},... | collective-permute-start | bytes 200 | tf_op jit(solution)/shard_map/ppermute | solution.py:402
  4.7 4.2 %collective-permute-start.171 = (s32[16]{0:T(128)S(1)}, s32[16]{0:T(128)S(1)}, u32[]{:S(2)}, u32[]{:S(2)}) collective-permute-start(s32[16]{0:T(128)S(1)} %pad_add_fusion.refs_0_), channel_id=1, source_target_pairs={{0,4},{4,8},{8,12},{12,0},{1,5},{5,9},{9,13},{13,1},{2,6},{6,10},{... | collective-permute-start | bytes 200 | tf_op jit(solution)/shard_map/ppermute | solution.py:402
  5.8 3.1 %copy-start.11 = (s32[16]{0:T(128)}, s32[16]{0:T(128)S(1)}, u32[]{:S(2)}) copy-start(s32[16]{0:T(128)S(1)} %collective-permute-done.173.refs_3_) | copy-start | bytes 196
  8.0 0.9 copy-start.12
  8.9 0.5 copy-start.13
  13.2 69.8 %copy-start = (bf16[2,8,1,1280]{3,1,2,0:T(8,128)(2,1)S(1)}, bf16[2,8,1,1280]{3,1,2,0:T(8,128)(2,1)}, u32[]{:S(2)}) copy-start(bf16[2,8,1,1280]{3,1,2,0:T(8,128)(2,1)} %param.110) | copy-start | bytes 122884
  13.2 69.8 %copy-start.1 = (bf16[2,8,1024]{2,1,0:T(8,128)(2,1)S(1)}, bf16[2,8,1024]{2,1,0:T(8,128)(2,1)}, u32[]{:S(2)}) copy-start(bf16[2,8,1024]{2,1,0:T(8,128)(2,1)} %gate_in.1) | copy-start | bytes 98308
  13.2 69.7 %copy-start.2 = (bf16[4,1,1280]{2,0,1:T(4,128)(2,1)S(1)}, bf16[4,1,1280]{2,0,1:T(4,128)(2,1)}, u32[]{:S(2)}) copy-start(bf16[4,1,1280]{2,0,1:T(4,128)(2,1)} %param.113) | copy-start | bytes 30724
  13.2 69.7 %copy-start.3 = (bf16[1,1280]{1,0:T(2,128)(2,1)S(1)}, bf16[1,1280]{1,0:T(2,128)(2,1)}, u32[]{:S(2)}) copy-start(bf16[1,1280]{1,0:T(2,128)(2,1)} %conv_bias.1) | copy-start | bytes 7684
  13.2 69.7 %copy-start.4 = (bf16[2,8,16]{2,1,0:T(8,128)(2,1)S(1)}, bf16[2,8,16]{2,1,0:T(8,128)(2,1)}, u32[]{:S(2)}) copy-start(bf16[2,8,16]{2,1,0:T(8,128)(2,1)} %dt_in.1) | copy-start | bytes 1540
  13.2 69.7 %copy-start.5 = (s32[4]{0:T(128)S(1)}, s32[4]{0:T(128)}, u32[]{:S(2)}) copy-start(s32[4]{0:T(128)} %live.3) | copy-start | bytes 52
  13.2 69.7 %copy-start.6 = (s32[8]{0:T(128)S(1)}, s32[8]{0:T(128)}, u32[]{:S(2)}) copy-start(s32[8]{0:T(128)} %get-tuple-element.556.arrival) | copy-start | bytes 100
  13.3 69.7 %copy-start.7 = (f32[16]{0:T(128)S(1)}, f32[16]{0:T(128)}, u32[]{:S(2)}) copy-start(f32[16]{0:T(128)} %param.115) | copy-start | bytes 196
  13.3 69.7 %copy-start.8 = (f32[16]{0:T(128)S(1)}, f32[16]{0:T(128)}, u32[]{:S(2)}) copy-start(f32[16]{0:T(128)} %param.116) | copy-start | bytes 196
  13.3 69.7 %copy-start.9 = (f32[16]{0:T(128)S(1)}, f32[16]{0:T(128)}, u32[]{:S(2)}) copy-start(f32[16]{0:T(128)} %param.117) | copy-start | bytes 196
  13.5 25.5 %collective-permute-start.165 = (bf16[4256,128]{1,0:T(8,128)(2,1)S(1)}, bf16[4256,128]{1,0:T(8,128)(2,1)}, u32[]{:S(2)}, u32[]{:S(2)}) collective-permute-start(bf16[4256,128]{1,0:T(8,128)(2,1)S(1)} %get-tuple-element.534), channel_id=1, source_target_pairs={{0,8},{4,12},{8,4},{12,0},{1,9},{5,13},{9,5},{13,1},{2,10},{6,14},... | collective-permute-start | bytes 3268616 | tf_op jit(solution)/shard_map/cond/branch_87_fun/ppermute | solution.py:434
  14.2 68.8 %collective-permute-start.166 = (bf16[4256,128]{1,0:T(8,128)(2,1)S(1)}, bf16[4256,128]{1,0:T(8,128)(2,1)}, u32[]{:S(2)}, u32[]{:S(2)}) collective-permute-start(bf16[4256,128]{1,0:T(8,128)(2,1)S(1)} %get-tuple-element.535), channel_id=1, source_target_pairs={{0,12},{8,0},{12,8},{1,13},{9,1},{13,9},{2,14},{10,2},{14,10},{3,1... | collective-permute-start | bytes 3268616 | tf_op jit(solution)/shard_map/cond/branch_87_fun/ppermute | solution.py:434
  88.4 9.9 %collective-permute-start.176 = (bf16[16,4096]{1,0:T(8,128)(2,1)S(1)}, bf16[16,4096]{1,0:T(8,128)(2,1)S(1)}, u32[]{:S(2)}, u32[]{:S(2)}) collective-permute-start(bf16[16,4096]{1,0:T(8,128)(2,1)S(1)} %get-tuple-element.562), channel_id=1, source_target_pairs={{0,3},{1,2},{2,1},{3,0},{4,7},{5,6},{6,5},{7,4},{8,11},{9,10},{10,... | collective-permute-start | bytes 393224 | tf_op jit(solution)/shard_map/ppermute | solution.py:486
  92.5 7.1 %collective-permute-start.175 = (bf16[16,4096]{1,0:T(8,128)(2,1)S(1)}, bf16[16,4096]{1,0:T(8,128)(2,1)S(1)}, u32[]{:S(2)}, u32[]{:S(2)}) collective-permute-start(bf16[16,4096]{1,0:T(8,128)(2,1)S(1)} %get-tuple-element.562), channel_id=1, source_target_pairs={{0,2},{1,3},{2,0},{3,1},{4,6},{5,7},{6,4},{7,5},{8,10},{9,11},{10,... | collective-permute-start | bytes 393224 | tf_op jit(solution)/shard_map/ppermute | solution.py:486
  92.8 6.8 %collective-permute-start.174 = (bf16[16,4096]{1,0:T(8,128)(2,1)S(1)}, bf16[16,4096]{1,0:T(8,128)(2,1)S(1)}, u32[]{:S(2)}, u32[]{:S(2)}) collective-permute-start(bf16[16,4096]{1,0:T(8,128)(2,1)S(1)} %get-tuple-element.562), channel_id=1, source_target_pairs={{0,1},{1,0},{2,3},{3,2},{4,5},{5,4},{6,7},{7,6},{8,9},{9,8},{10,11... | collective-permute-start | bytes 393224 | tf_op jit(solution)/shard_map/ppermute | solution.py:486

commit v2 on v1

--- a/solution.py
+++ b/solution.py
@@ -33,21 +33,88 @@
     return graphs
 
 
+def parts_of(value, count):
+    out = []
+    for _ in range(count):
+        part = value.astype(BF16).astype(F32)
+        out.append(part)
+        value = value - part
+    return out
+
+
+def sum_of_parts(rows, count):
+    size = rows.shape[0] // count
+    total = rows[:size]
+    for part in range(1, count):
+        total = total + rows[part * size : (part + 1) * size]
+    return total
+
+
+def silu(value):
+    return value / (1.0 + jnp.exp(-value))
+
+
+def softplus(value):
+    return jnp.maximum(value, 0.0) + jnp.log1p(jnp.exp(-jnp.abs(value)))
+
+
+def prepare(small, wide, scale, gate, begun, gains):
+    dt, tokens, gates, weights, bias, dt_shift, rates, skips, norms = small
+    slots, heads = scale.shape
+    span = wide.shape[1]
+    steps, kept = [], []
+    for step in range(2):
+        steps.append(softplus(dt[step] + dt_shift))
+        kept.append(jnp.exp(steps[step] * -jnp.exp(rates)))
+    scale[...] = kept[0] * kept[1]
+    per_head = jnp.concatenate(steps + kept + [jnp.broadcast_to(skips, (slots, heads))], axis=0)
+    head_of = lax.div(lax.broadcasted_iota(jnp.int32, (heads, span), 1), span // heads)
+    spread = jnp.where(
+        head_of == lax.broadcasted_iota(jnp.int32, (heads, span), 0), 1.0, 0.0
+    ).astype(BF16)
+    wide[...] = sum_of_parts(
+        jnp.dot(
+            jnp.concatenate(parts_of(per_head, 3), axis=0).astype(BF16),
+            spread,
+            preferred_element_type=F32,
+        ),
+        3,
+    )
+    taps = weights.shape[0] - 1
+    begun[0] = tokens[0] * weights[taps : taps + 1] + bias
+    begun[1] = tokens[0] * weights[taps - 1 : taps] + tokens[1] * weights[taps : taps + 1] + bias
+    for step in range(2):
+        gate[step] = silu(gates[step])
+    gains[...] = jnp.concatenate([norms[k : k + 1] for k in range(norms.shape[0])], axis=1)
+
+
 def route_kernel(graphs, replicas, slots, *refs):
-    metas = refs[:replicas]
-    states, windows, buf_a, buf_b, branch, arrival, win_rows, sems = refs[replicas:]
+    to_replica, to_slot, *others = refs[: replicas + 1]
+    states, *refs = refs[replicas + 1 :]
+    count = (len(refs) - 3 - 9) // 2
+    small, refs, held = refs[:count], refs[count:-count], refs[-count:]
+    buf_a, buf_b, branch, loops, wide, scale, gate, begun, gains, win_rows, sems, small_sems = refs
+    windows = held[0]
+    fetches = [
+        pltpu.make_async_copy(source, target, small_sems.at[k])
+        for k, (source, target) in enumerate(zip(small, held))
+    ]
+    for fetch in fetches:
+        fetch.start()
     half = slots // 2
     span = states.shape[1]
-    taps = windows.shape[0]
+    taps = held[0].shape[0]
     lanes = states.shape[2]
     block = win_rows.shape[1]
     me = lax.axis_index("replica")
     sources = [lax.rem(me + (replicas - k), replicas) for k in range(replicas)]
-    code = jnp.int32(0)
-    for k in range(replicas):
-        edges = jnp.int32(0)
-        for i in range(slots):
-            edges = edges + jnp.left_shift(jnp.int32(1), metas[k][i])
+    edges = jnp.int32(0)
+    for i in range(slots):
+        edges = edges + jnp.left_shift(jnp.int32(1), to_replica[i])
+    code = jnp.left_shift(lax.div(edges, jnp.int32(half)), me * replicas)
+    for k, other in enumerate(others, 1):
+        flags = jnp.left_shift(jnp.int32(1), other[...]).astype(F32)
+        edges = jnp.sum(flags).astype(jnp.int32)
         code = code + jnp.left_shift(lax.div(edges, jnp.int32(half)), sources[k] * replicas)
     index = jnp.int32(0)
     bits = jnp.int32(0)
@@ -73,7 +140,7 @@
     counts = [jnp.int32(0), jnp.int32(0)]
     picked = []
     for i in range(slots):
-        which = second_matching(me, metas[0][i])
+        which = second_matching(me, to_replica[i])
         place = jnp.where(which == 0, counts[0], counts[1])
         counts = [counts[0] + (1 - which), counts[1] + which]
         picked.append((which, place))
@@ -83,205 +150,169 @@
             def _(buf=buf, i=i, place=place):
                 pack(buf, place, i).start()
 
-    for k in range(replicas):
-        which = second_matching(sources[k], me)
-        base = which * half + (2 * half if k == 0 else 0)
-        count = jnp.int32(0)
-        for i in range(slots):
-            mine = metas[k][i] == me
-
-            @pl.when(mine)
-            def _(k=k, i=i, base=base, count=count):
-                arrival[metas[k][slots + i]] = base + count
-
-            count = count + jnp.where(mine, 1, 0)
+    loop = lax.bitwise_and(lax.shift_right_logical(code, me * replicas + me), jnp.int32(1))
+    second = second_matching(me, me)
+    loops[0] = loop * (1 - second)
+    loops[1] = loop * second
 
     win_rows[...] = jnp.zeros_like(win_rows)
+    for fetch in fetches:
+        fetch.wait()
     for tap in range(taps):
         tokens = windows[tap].astype(F32)
         for i in range(slots):
             which, place = picked[i]
             win_rows[which, pl.ds(tap * half + place, 1), :] = tokens[i : i + 1]
+    for i in range(slots):
+        which, place = picked[i]
+        win_rows[which, pl.ds(taps * half + place, 1), :] = jnp.full(
+            (1, win_rows.shape[2]), to_slot[i].astype(F32)
+        )
     for m, buf in enumerate((buf_a, buf_b)):
         rows = win_rows[m].astype(BF16)
         for part in range(rows.shape[1] // lanes):
             top = half * span + part * block
             buf[top : top + block, :] = rows[:, part * lanes : (part + 1) * lanes]
 
+    prepare([ref[...].astype(F32) for ref in held[1:]], wide, scale, gate, begun, gains)
+
     for i in range(slots):
-        which, place = picked[i]
-        for m, buf in enumerate((buf_a, buf_b)):
-
-            @pl.when(which == m)
-            def _(buf=buf, i=i, place=place):
-                pack(buf, place, i).wait()
-
-
-def parts_of(value, count):
-    out = []
-    for _ in range(count):
-        part = value.astype(BF16).astype(F32)
-        out.append(part)
-        value = value - part
-    return out
-
-
-def sum_of_parts(rows, count):
-    size = rows.shape[0] // count
-    total = rows[:size]
-    for part in range(1, count):
-        total = total + rows[part * size : (part + 1) * size]
-    return total
-
-
-def silu(value):
-    return value / (1.0 + jnp.exp(-value))
-
-
-def softplus(value):
-    return jnp.maximum(value, 0.0) + jnp.log1p(jnp.exp(-jnp.abs(value)))
-
-
-def row_copy(arrival, sources, held, sems, row, act):
-    slots, span, _ = held.shape
-    half = slots // 2
-    place = arrival[row]
-    which = lax.div(place, half)
-    rows = pl.ds(pl.multiple_of(lax.rem(place, half) * span, span), span)
-    for m, source in enumerate(sources):
-
-        @pl.when(which == m)
-        def _(source=source):
-            act(pltpu.make_async_copy(source.at[rows], held.at[row], sems.at[row]))
+        pack(buf_a, 0, i).wait()
+
+
+def fetch_rows(loops, pairs, held, sems):
+    _, span, _ = held.shape
+    half = held.shape[0] // 2
+    for m, sources in enumerate(pairs):
+        for own, source in enumerate(sources):
+
+            @pl.when(loops[m] == own)
+            def _(m=m, source=source):
+                for member in range(half):
+                    row = m * half + member
+                    pltpu.make_async_copy(
+                        source.at[pl.ds(member * span, span)], held.at[row], sems.at[row]
+                    ).start()
+
+
+def row_wait(pairs, held, sems, row):
+    rows = pl.ds(0, held.shape[1])
+    pltpu.make_async_copy(pairs[0][0].at[rows], held.at[row], sems.at[row]).wait()
 
 
 def mix_kernel(
-    arrival,
+    loops,
     live,
     got_a,
     got_b,
     own_a,
     own_b,
-    conv_in,
-    gate_in,
-    dt_in,
+    wide,
+    gate,
+    begun,
     conv_weight,
-    conv_bias,
-    dt_bias,
-    a_log,
-    skip_gain,
     norm_gain,
     out_weight,
     partial,
     updates,
     inputs,
-    scale,
     last_window,
+    order,
     held,
+    win_held,
     weight_held,
-    win_held,
-    win_all,
-    win_rows,
     in_sem,
     win_sem,
     weight_sem,
 ):
     slots, span, state = held.shape
-    heads = dt_in.shape[2]
     half = slots // 2
-    taps = win_rows.shape[0]
+    taps = conv_weight.shape[0] - 1
+    pairs = ((got_a, own_a), (got_b, own_b))
+    win_size = win_held.shape[1]
+    block = win_size // (begun.shape[2] // state)
+
+    for m, sources in enumerate(pairs):
+        for own, source in enumerate(sources):
+
+            @pl.when(loops[m] == own)
+            def _(m=m, source=source):
+                pltpu.make_async_copy(
+                    source.at[pl.ds(half * span, win_size)], win_held.at[m], win_sem.at[m]
+                ).start()
+
+    fetch_rows(loops, pairs, held, in_sem)
     chunk = out_weight.shape[0] // weight_sem.shape[0]
-    sources = (got_a, got_b, own_a, own_b)
-    win_size = win_held.shape[1]
-    block = win_all.shape[1]
-
-    def win_copy(m):
-        return pltpu.make_async_copy(
-            sources[m].at[pl.ds(half * span, win_size)], win_held.at[m], win_sem.at[m]
-        )
-
-    def weight_copy(part):
+    fetches = []
+    for part in range(weight_sem.shape[0]):
         rows = pl.ds(part * chunk, chunk)
-        return pltpu.make_async_copy(
-            out_weight.at[rows], weight_held.at[rows], weight_sem.at[part]
-        )
-
-    for m in range(len(sources)):
-        win_copy(m).start()
-    for row in range(slots):
-        row_copy(arrival, sources, held, in_sem, row, lambda copy: copy.start())
-    for part in range(weight_sem.shape[0]):
-        weight_copy(part).start()
-
-    steps, kept = [], []
+        fetches.append(
+            pltpu.make_async_copy(out_weight.at[rows], weight_held.at[rows], weight_sem.at[part])
+        )
+        fetches[part].start(priority=1)
+
+    for m in range(len(pairs)):
+        pltpu.make_async_copy(
+            got_a.at[pl.ds(half * span, win_size)], win_held.at[m], win_sem.at[m]
+        ).wait()
+    parts = []
+    for part in range(win_size // block):
+        cut = slice(part * block, (part + 1) * block)
+        parts.append(jnp.concatenate([win_held[m, cut, :] for m in range(len(pairs))], axis=0))
+    top = taps * half
+    arrived = [parts[0][m * block + top : m * block + top + half].astype(F32) for m in range(len(pairs))]
+    order[...] = jnp.concatenate(arrived, axis=0)
+    shape = (len(pairs) * block, taps * slots)
+    column = lax.broadcasted_iota(jnp.int32, shape, 1)
+    tap_of = lax.div(lax.rem(lax.broadcasted_iota(jnp.int32, shape, 0), block), half)
+    slot_at = jnp.concatenate(
+        [rows[:, : taps * slots] for rows in arrived for _ in range(block // half)], axis=0
+    )
+    choose = jnp.where(
+        (tap_of == lax.div(column, slots)) & (slot_at == lax.rem(column, slots).astype(F32)),
+        1.0,
+        0.0,
+    ).astype(BF16)
+    windows = lax.dot_general(
+        choose,
+        jnp.concatenate(parts, axis=1),
+        (((0,), (0,)), ((), ())),
+        preferred_element_type=F32,
+    )
+    line = [windows[tap * slots : (tap + 1) * slots] for tap in range(taps)]
+    last_window[...] = line[taps - 1]
+
+    weights = conv_weight[...].astype(F32)
+    acts = []
     for step in range(2):
-        steps.append(softplus(dt_in[step].astype(F32) + dt_bias[...]))
-        kept.append(jnp.exp(steps[step] * -jnp.exp(a_log[...])))
-    scale[...] = kept[0] * kept[1]
-    per_head = jnp.concatenate(
-        steps + kept + [jnp.broadcast_to(skip_gain[...], (slots, heads))], axis=0
-    )
-    head_of = lax.div(lax.broadcasted_iota(jnp.int32, (heads, span), 1), span // heads)
-    spread = jnp.where(
-        head_of == lax.broadcasted_iota(jnp.int32, (heads, span), 0), 1.0, 0.0
-    ).astype(BF16)
-    wide = sum_of_parts(
-        jnp.dot(
-            jnp.concatenate(parts_of(per_head, 3), axis=0).astype(BF16),
-            spread,
-            preferred_element_type=F32,
-        ),
-        3,
-    )
+        total = begun[step]
+        for tap in range(taps - step):
+            total = total + line[step + tap] * weights[tap : tap + 1]
+        acts.append(silu(total))
+    xs = [act[:, :span] for act in acts]
+    bs = [act[:, span : span + state] for act in acts]
+    cs = [act[:, span + state :] for act in acts]
     step_size = [wide[:slots], wide[slots : 2 * slots]]
     retained = [wide[2 * slots : 3 * slots], wide[3 * slots : 4 * slots]]
     skip = wide[4 * slots :]
-
-    for m in range(len(sources)):
-        win_copy(m).wait()
-        for part in range(win_size // block):
-            win_all[m, :, part * state : (part + 1) * state] = win_held[
-                m, part * block : (part + 1) * block, :
-            ].astype(F32)
-    for row in range(slots):
-        place = arrival[row]
-        which = lax.div(place, half)
-        member = lax.rem(place, half)
-        for tap in range(taps):
-            win_rows[tap, row : row + 1, :] = win_all[
-                which, pl.ds(tap * half + member, 1), :
-            ]
-    last_window[...] = win_rows[taps - 1]
-
-    line = [win_rows[tap] for tap in range(taps)] + [
-        conv_in[0].astype(F32),
-        conv_in[1].astype(F32),
-    ]
-    weights = conv_weight[...].astype(F32)
-    acts = []
-    for step in range(2):
-        total = line[step] * weights[0:1]
-        for tap in range(1, taps + 1):
-            total = total + line[step + tap] * weights[tap : tap + 1]
-        acts.append(silu(total + conv_bias[...].astype(F32)))
-    xs = [act[:, :span] for act in acts]
-    bs = [act[:, span : span + state] for act in acts]
-    cs = [act[:, span + state :] for act in acts]
     us = [step_size[0] * xs[0], step_size[1] * xs[1]]
     updates[0] = retained[1] * us[0]
     updates[1] = us[1]
     inputs[0] = bs[0]
     inputs[1] = bs[1]
     queries = jnp.concatenate(parts_of(jnp.concatenate(cs, axis=0), 3), axis=0).astype(BF16)
-    row_of = lax.rem(lax.broadcasted_iota(jnp.int32, (2 * slots, span), 0), slots)
+    row_of = lax.rem(lax.broadcasted_iota(jnp.int32, (2 * slots, span), 0), slots).astype(F32)
+    slot_of = jnp.concatenate(arrived, axis=0)[:, :1]
 
     ys = jnp.zeros((2 * slots, span), F32)
     for row in range(slots):
-        row_copy(arrival, sources, held, in_sem, row, lambda copy: copy.wait())
+        if row % (slots // 2) == 0:
+            for later in range(row, row + (slots // 2)):
+                row_wait(pairs, held, in_sem, later)
         got = lax.dot_general(
             queries, held[row], (((1,), (1,)), ((), ())), preferred_element_type=F32
         )
-        ys = jnp.where(row_of == row, sum_of_parts(got, 3), ys)
+        ys = jnp.where(row_of == slot_of[row : row + 1], sum_of_parts(got, 3), ys)
 
     def dots(b, c):
         return jnp.sum(b * c, axis=1, keepdims=True)
@@ -292,18 +323,18 @@
         + us[1] * dots(bs[1], cs[1])
         + skip * xs[1],
     ]
-    gains = norm_gain[...].astype(F32)
+    gains = norm_gain[...]
     normed = []
     for step in range(2):
-        gated = reads[step] * silu(gate_in[step].astype(F32))
+        gated = reads[step] * gate[step]
         factor = lax.rsqrt(jnp.sum(gated * gated, axis=1, keepdims=True) * (1.0 / span) + 1e-05)
         normed.append((gated * factor) * gains)
     normed = jnp.concatenate(normed, axis=0)
-    alive = live[lax.axis_index("replica")]
+    alive = live[lax.axis_index("replica")].astype(F32)
     normed = jnp.where(row_of < alive, normed, 0.0).astype(BF16)
     total = None
-    for part in range(weight_sem.shape[0]):
-        weight_copy(part).wait()
+    for part, fetch in enumerate(fetches):
+        fetch.wait()
         cut = slice(part * chunk, (part + 1) * chunk)
         term = jnp.dot(normed[:, cut], weight_held[cut, :], preferred_element_type=F32)
         total = term if total is None else total + term
@@ -311,7 +342,7 @@
 
 
 def state_kernel(
-    arrival,
+    loops,
     live,
     got_a,
     got_b,
@@ -321,6 +352,7 @@
     inputs,
     scale,
     last_window,
+    order,
     conv_in,
     states_out,
     windows_out,
@@ -332,9 +364,9 @@
     slots, span, state = held.shape
     heads = scale.shape[1]
     width = span // heads
-    sources = (got_a, got_b, own_a, own_b)
-    for row in range(slots):
-        row_copy(arrival, sources, held, in_sem, row, lambda copy: copy.start())
+    pairs = ((got_a, own_a), (got_b, own_b))
+    fetch_rows(loops, pairs, held, in_sem)
+    slot_of = [jnp.max(order[row : row + 1, :]).astype(jnp.int32) for row in range(slots)]
     alive = live[lax.axis_index("replica")]
     keep = lax.broadcasted_iota(jnp.int32, last_window.shape, 0) < alive
     for tap, tokens in enumerate(
@@ -352,20 +384,24 @@
     b_rows = jnp.concatenate(b_parts, axis=0)
     b_of = lax.rem(lax.broadcasted_iota(jnp.int32, b_rows.shape, 0), slots)
     for row in range(slots):
-        row_copy(arrival, sources, held, in_sem, row, lambda copy: copy.wait())
+        slot = slot_of[row]
+        factors = scale[pl.ds(slot, 1), :]
+        if row % (slots // 2) == 0:
+            for later in range(row, row + (slots // 2)):
+                row_wait(pairs, held, in_sem, later)
         added = jnp.dot(
             u_columns,
-            jnp.where(b_of == row, b_rows, 0.0).astype(BF16),
+            jnp.where(b_of == slot, b_rows, 0.0).astype(BF16),
             preferred_element_type=F32,
         )
         for head in range(heads):
             rows = slice(head * width, (head + 1) * width)
             value = (
-                scale[row : row + 1, head : head + 1] * held[row, rows, :].astype(F32)
+                factors[:, head : head + 1] * held[row, rows, :].astype(F32)
                 + added[rows]
             )
-            held_out[row, rows, :] = jnp.where(row < alive, value, 0.0).astype(BF16)
-        pltpu.make_async_copy(held_out.at[row], states_out.at[row], out_sem.at[row]).start()
+            held_out[row, rows, :] = jnp.where(slot < alive, value, 0.0).astype(BF16)
+        pltpu.make_async_copy(held_out.at[row], states_out.at[slot], out_sem.at[row]).start()
     for row in range(slots):
         pltpu.make_async_copy(held_out.at[row], states_out.at[row], out_sem.at[row]).wait()
 
@@ -394,12 +430,12 @@
     taps, channels = conv_state.shape[1], conv_state.shape[3]
     columns = out_weight.shape[1]
     graphs = send_graphs(replicas)
-    block = 16 * pl.cdiv(half * taps, 16)
+    block = 16 * pl.cdiv(half * (taps + 1), 16)
     win_size = block * (channels // state)
 
-    meta = jnp.concatenate([dst_replica, dst_slot])
-    metas = [meta] + [
-        lax.ppermute(meta, "replica", [(s, (s + k) % replicas) for s in range(replicas)])
+    mine = dst_replica.reshape(1, slots)
+    others = [
+        lax.ppermute(mine, "replica", [(s, (s + k) % replicas) for s in range(replicas)])
         for k in range(1, replicas)
     ]
     tokens = conv_in.reshape(2, slots, channels)
@@ -408,23 +444,44 @@
     smem = pl.BlockSpec(memory_space=SMEM)
     vmem = pl.BlockSpec(memory_space=VMEM)
     packed = jax.ShapeDtypeStruct((half * span + win_size, state), BF16)
-    own_a, own_b, branch, arrival = pl.pallas_call(
+    weights = conv_weight.reshape(taps + 1, channels)
+    lanes = 128
+    small = (
+        jnp.swapaxes(conv_state, 0, 1).reshape(taps, slots, channels),
+        dt_in,
+        tokens,
+        gate_in,
+        weights,
+        conv_bias,
+        dt_bias.reshape(1, heads),
+        a_log.reshape(1, heads),
+        skip_gain.reshape(1, heads),
+        norm_gain.reshape(span // lanes, lanes),
+    )
+    f32 = lambda *shape: jax.ShapeDtypeStruct(shape, F32)
+    own_a, own_b, branch, loops, wide, scale, gate, begun, gains = pl.pallas_call(
         functools.partial(route_kernel, graphs, replicas, slots),
         out_shape=(
             packed,
             packed,
             jax.ShapeDtypeStruct((1,), jnp.int32),
-            jax.ShapeDtypeStruct((slots,), jnp.int32),
+            jax.ShapeDtypeStruct((2,), jnp.int32),
+            f32(5 * slots, span),
+            f32(slots, heads),
+            f32(2, slots, span),
+            f32(2, slots, channels),
+            f32(1, span),
         ),
-        in_specs=[smem] * replicas + [any_spec, vmem],
-        out_specs=(vmem, vmem, smem, smem),
-        scratch_shapes=[VMEM((2, block, channels), F32), pltpu.SemaphoreType.DMA((slots,))],
+        in_specs=[smem] * 2 + [vmem] * (replicas - 1) + [any_spec] * (1 + len(small)),
+        out_specs=(vmem, vmem, smem, smem) + (vmem,) * 5,
+        scratch_shapes=[
+            VMEM((2, block, channels), F32),
+            pltpu.SemaphoreType.DMA((slots,)),
+            pltpu.SemaphoreType.DMA((len(small),)),
+        ]
+        + [VMEM(value.shape, value.dtype) for value in small],
         name="route",
-    )(
-        *metas,
-        ssm_state.reshape(slots, span, state),
-        jnp.swapaxes(conv_state, 0, 1).reshape(taps, slots, channels),
-    )
+    )(dst_replica, dst_slot, *others, ssm_state.reshape(slots, span, state), *small)
 
     def along(first, second):
         def send(rows_a, rows_b):
@@ -441,43 +498,36 @@
     )
     arrived = (got_a, got_b, own_a, own_b)
 
-    weight_parts = 4
-    partial, updates, inputs, scale, last_window = pl.pallas_call(
+    partial, updates, inputs, last_window, order = pl.pallas_call(
         mix_kernel,
         out_shape=(
             jax.ShapeDtypeStruct((2 * slots, columns), BF16),
             jax.ShapeDtypeStruct((2, slots, span), F32),
             jax.ShapeDtypeStruct((2, slots, state), F32),
-            jax.ShapeDtypeStruct((slots, heads), F32),
             jax.ShapeDtypeStruct((slots, channels), F32),
+            jax.ShapeDtypeStruct((slots, state), F32),
         ),
-        in_specs=[smem, smem] + [any_spec] * 4 + [vmem] * 9 + [any_spec],
+        in_specs=[smem, smem] + [any_spec] * 4 + [vmem] * 5 + [any_spec],
         out_specs=(vmem,) * 5,
         scratch_shapes=[
             VMEM((slots, span, state), BF16),
+            VMEM((2, win_size, state), BF16),
             VMEM(out_weight.shape, BF16),
-            VMEM((4, win_size, state), BF16),
-            VMEM((4, block, channels), F32),
-            VMEM((taps, slots, channels), F32),
             pltpu.SemaphoreType.DMA((slots,)),
-            pltpu.SemaphoreType.DMA((4,)),
-            pltpu.SemaphoreType.DMA((weight_parts,)),
+            pltpu.SemaphoreType.DMA((2,)),
+            pltpu.SemaphoreType.DMA((8,)),
         ],
         compiler_params=pltpu.CompilerParams(vmem_limit_bytes=52 * 2**20),
         name="mix",
     )(
-        arrival,
+        loops,
         live,
         *arrived,
-        tokens,
-        gate_in,
-        dt_in,
-        conv_weight.reshape(taps + 1, channels),
-        conv_bias,
-        dt_bias.reshape(1, heads),
-        a_log.reshape(1, heads),
-        skip_gain.reshape(1, heads),
-        norm_gain.reshape(1, span),
+        wide,
+        gate,
+        begun,
+        weights,
+        gains,
         out_weight,
     )
 
@@ -492,7 +542,7 @@
             jax.ShapeDtypeStruct((slots, span, state), BF16),
             jax.ShapeDtypeStruct((taps, slots, channels), BF16),
         ),
-        in_specs=[smem, smem] + [any_spec] * 4 + [vmem] * 5,
+        in_specs=[smem, smem] + [any_spec] * 4 + [vmem] * 6,
         out_specs=(any_spec, vmem),
         scratch_shapes=[
             VMEM((slots, span, state), BF16),
@@ -500,14 +550,14 @@
             pltpu.SemaphoreType.DMA((slots,)),
             pltpu.SemaphoreType.DMA((slots,)),
         ],
-        compiler_params=pltpu.CompilerParams(vmem_limit_bytes=32 * 2**20),
+        compiler_params=pltpu.CompilerParams(vmem_limit_bytes=52 * 2**20),
         cost_estimate=pl.CostEstimate(
             flops=40 * slots * span * state,
             bytes_accessed=4 * slots * span * state,
             transcendentals=0,
         ),
         name="states",
-    )(arrival, live, *arrived, updates, inputs, scale, last_window, tokens)
+    )(loops, live, *arrived, updates, inputs, scale, last_window, order, tokens)
 
     terms = [term.astype(F32) for term in terms]
     while len(terms) > 1:

time: 101 us -> 78.1 us (0.77)
  waiting for transfers between devices: 68.5 us -> 54 us
  starting transfers between devices: 13.7 us -> 6.66 us
  Pallas kernels: 13.7 us -> 12.2 us
    ppermute x2 -> x1, waiting for transfers between devices: 64.2 us -> 47.6 us  [send(): out.append(lax.ppermute(value, 'replica', moves) if moves else value)]
    ppermute x2 -> x1, starting transfers between devices: 5.21 us -> 0.63 us  [send(): out.append(lax.ppermute(value, 'replica', moves) if moves else value)]
    ppermute x3, starting transfers between devices: 4.66 us -> 2.21 us  [routed(): lax.ppermute(partial, 'tensor', [(i, i ^ k) for i in range(members)])]
    pallas_call x1, Pallas kernels: 5.25 us -> 3.88 us  [routed(): pl.pallas_call(state_kernel, out_shape=(jax.ShapeDtypeStruct((slots, span...]
    ppermute x3, waiting for transfers between devices: 1.33 us -> 2.47 us  [routed(): lax.ppermute(partial, 'tensor', [(i, i ^ k) for i in range(members)])]
  transfers between devices with their start and end apart: 8 -> 7, of which waited for: 5 -> 5; matrix products, arithmetic and copies ran while one was open for 1% -> 1% of each run, Pallas kernels for 5% -> 5%
where the time goes in v2:
time: 78.1 us; the launch traced here: 76.5 us
  waiting for transfers between devices  54 us (69%)
  Pallas kernels  12.2 us (16%)
  starting transfers between devices  6.66 us (9%)
  local copies, waits for them, and re-layouts  1.53 us (2%)
  between operations  1.36 us (2%)
    ppermute x1, waiting for transfers between devices, send(): out.append(lax.ppermute(value, 'replica', moves) if moves else value)  47.6 us
    pallas_call x1, Pallas kernels, routed(): pl.pallas_call(mix_kernel, out_shape=(jax.ShapeDtypeStruct((2 * slots, co...  4.83 us
    pallas_call x1, Pallas kernels, routed(): pl.pallas_call(state_kernel, out_shape=(jax.ShapeDtypeStruct((slots, span...  3.88 us
    ppermute x3, waiting for transfers between devices, routed(): lax.ppermute(mine, 'replica', [(s, (s + k) % replicas) for s in range(rep...  3.87 us
    ppermute x3, starting transfers between devices, routed(): lax.ppermute(mine, 'replica', [(s, (s + k) % replicas) for s in range(rep...  3.83 us
    pallas_call x1, Pallas kernels, routed(): pl.pallas_call(functools.partial(route_kernel, graphs, replicas, slots),...  3.53 us
    ppermute x3, waiting for transfers between devices, routed(): lax.ppermute(partial, 'tensor', [(i, i ^ k) for i in range(members)])  2.47 us
    ppermute x3, starting transfers between devices, routed(): lax.ppermute(partial, 'tensor', [(i, i ^ k) for i in range(members)])  2.21 us
  transfers between devices with their start and end apart: 7, of which 5 were waited for; matrix products, arithmetic and copies ran while one was open for 1% of the time, Pallas kernels for 5%

profile of v2, /device:TPU:5, one launch (start us, length us, event | category | flops | bytes accessed | tf_op | source)
XLA Modules:
  0.0 76.5 jit_solution(2123101428879655658)
XLA Ops:
  0.6 3.4 %collective-permute-start.173 = (s32[1,8]{1,0:T(1,128)}, s32[1,8]{1,0:T(1,128)S(1)}, u32[]{:S(2)}, u32[]{:S(2)}) collective-permute-start(s32[1,8]{1,0:T(1,128)} %bitcast.29), channel_id=1, source_target_pairs={{0,12},{4,0},{8,4},{12,8},{1,13},{5,1},{9,5},{13,9},{2,14},{6,2},{... | collective-permute-start | bytes 104 | tf_op jit(solution)/shard_map/ppermute | solution.py:438
  4.0 0.5 collective-permute-start.171
  4.5 0.4 collective-permute-done.173.refs_4_
  4.9 2.6 %collective-permute-done.172.refs_3_ = s32[1,8]{1,0:T(1,128)S(1)} collective-permute-done((s32[1,8]{1,0:T(1,128)}, s32[1,8]{1,0:T(1,128)S(1)}, u32[]{:S(2)}, u32[]{:S(2)}) %collective-permute-start.172) | collective-permute-done | bytes 64 | tf_op jit(solution)/shard_map/ppermute | solution.py:438
  7.4 0.9 %collective-permute-done.171.refs_2_ = s32[1,8]{1,0:T(1,128)S(1)} collective-permute-done((s32[1,8]{1,0:T(1,128)}, s32[1,8]{1,0:T(1,128)S(1)}, u32[]{:S(2)}, u32[]{:S(2)}) %collective-permute-start.171) | collective-permute-done | bytes 64 | tf_op jit(solution)/shard_map/ppermute | solution.py:438
  8.3 0.5 copy-done.11
  8.8 3.5 %route.1 = (bf16[4256,128]{1,0:T(8,128)(2,1)S(1)}, bf16[4256,128]{1,0:T(8,128)(2,1)S(1)}, s32[1]{0:T(128)}, s32[2]{0:T(128)}, f32[40,1024]{1,0:T(8,128)}, /*inde...) custom-call(s32[8]{0:T(128)} %refs_0_.1, s32[8]{0:T(128)} %refs_1_.1, ...), custom_call_target="tpu_custom_call" | custom-call | tf_op jit(solution)/shard_map/route/pallas_call | solution.py:462
  12.9 0.0 copy-start.1
  12.9 0.0 copy-start.2
  13.0 0.0 copy-start.4
  13.0 0.0 copy-start.7
  13.0 49.3 %conditional.1 = (bf16[4256,128]{1,0:T(8,128)(2,1)}, bf16[4256,128]{1,0:T(8,128)(2,1)}) conditional(s32[]{:T(128)} %bitcast.11, (bf16[4256,128]{1,0:T(8,128)(2,1)S(1)}, bf16[4256,128]{1,0:T(8,128)(2,1)S(1)}) %tuple.368, (bf16[4256,128]{1,0:T(8,128)(2,1)S(1)}, bf16[4256,128]{1,0:T(8,128)(2,1)S(1)}) %tuple.369, ...), branch_computations={%region_0.0_spmd, %region_1.0_spmd, %region_2.0_spmd, %region_3.0_... | conditional | bytes 8716384 | solution.py:496
  13.1 0.6 collective-permute-start.42
  13.7 1.0 %copy.66 = bf16[4256,128]{1,0:T(8,128)(2,1)} copy(bf16[4256,128]{1,0:T(8,128)(2,1)S(1)} %get-tuple-element.628) | data formatting | bytes 2179072 | tf_op jit(solution)/shard_map/cond
  14.7 47.6 %collective-permute-done.42 = bf16[4256,128]{1,0:T(8,128)(2,1)} collective-permute-done((bf16[4256,128]{1,0:T(8,128)(2,1)S(1)}, bf16[4256,128]{1,0:T(8,128)(2,1)}, u32[]{:S(2)}, u32[]{:S(2)}) %collective-permute-start.42) | collective-permute-done | bytes 1089568 | tf_op jit(solution)/shard_map/cond/branch_23_fun/ppermute | solution.py:491
  62.4 0.0 copy-start
  62.4 0.0 copy-start.5
  62.4 4.8 %mix.1 = (bf16[16,4096]{1,0:T(8,128)(2,1)S(1)}, f32[2,8,1024]{2,1,0:T(8,128)S(1)}, f32[2,8,128]{2,1,0:T(8,128)S(1)}, f32[8,1280]{1,0:T(8,128)S(1)}, f32[8,128]{1,0:T(8,128)S(1)}) custom-call(s32[2]{0:T(128)S(1)} %copy-done.8, s32[4]{0:T(128)S(1)} %copy-done.7, bf16[4256,128]{1,0:T(8,128)(2,1)} %get-tuple-element.565.got_a, ...), custom_call_target="tpu_custom_call" | custom-call | tf_op jit(solution)/shard_map/mix/pallas_call | solution.py:501
  67.2 1.7 %collective-permute-start.176 = (bf16[16,4096]{1,0:T(8,128)(2,1)S(1)}, bf16[16,4096]{1,0:T(8,128)(2,1)S(1)}, u32[]{:S(2)}, u32[]{:S(2)}) collective-permute-start(bf16[16,4096]{1,0:T(8,128)(2,1)S(1)} %get-tuple-element.571), channel_id=1, source_target_pairs={{0,3},{1,2},{2,1},{3,0},{4,7},{5,6},{6,5},{7,4},{8,11},{9,10},{10,... | collective-permute-start | bytes 393224 | tf_op jit(solution)/shard_map/ppermute | solution.py:536
  68.9 0.3 collective-permute-start.175
  69.1 0.3 collective-permute-start.174
  69.5 3.9 %states.1 = (bf16[8,1024,128]{2,1,0:T(8,128)(2,1)}, bf16[3,8,1280]{2,1,0:T(8,128)(2,1)}) custom-call(s32[2]{0:T(128)S(1)} %copy-done.8, s32[4]{0:T(128)S(1)} %copy-done.7, bf16[4256,128]{1,0:T(8,128)(2,1)} %get-tuple-element.565.got_a, bf16[4256,128]{1,0:T(8,128)(2,1)} %get-tuple-element.566.got_b, bf16[4256,128]{1,0:T(8,128)(2,1)S(1)} %get-tuple-element.564.own_a, ...), custom_call_target="tpu_custom_call" | custom-call | flops 41943040 | bytes 4194304 | tf_op jit(solution)/shard_map/states/pallas_call | solution.py:539
  73.3 2.5 %collective-permute-done.175 = bf16[16,4096]{1,0:T(8,128)(2,1)S(1)} collective-permute-done((bf16[16,4096]{1,0:T(8,128)(2,1)S(1)}, bf16[16,4096]{1,0:T(8,128)(2,1)S(1)}, u32[]{:S(2)}, u32[]{:S(2)}) %collective-permute-start.175) | collective-permute-done | bytes 131104 | tf_op jit(solution)/shard_map/ppermute | solution.py:536
  75.8 0.7 fusion
  (20 shorter events, 0.0 us)
Async XLA Ops:
  0.6 4.2 %collective-permute-start.173 = (s32[1,8]{1,0:T(1,128)}, s32[1,8]{1,0:T(1,128)S(1)}, u32[]{:S(2)}, u32[]{:S(2)}) collective-permute-start(s32[1,8]{1,0:T(1,128)} %bitcast.29), channel_id=1, source_target_pairs={{0,12},{4,0},{8,4},{12,8},{1,13},{5,1},{9,5},{13,9},{2,14},{6,2},{... | collective-permute-start | bytes 104 | tf_op jit(solution)/shard_map/ppermute | solution.py:438
  4.0 3.4 %collective-permute-start.172 = (s32[1,8]{1,0:T(1,128)}, s32[1,8]{1,0:T(1,128)S(1)}, u32[]{:S(2)}, u32[]{:S(2)}) collective-permute-start(s32[1,8]{1,0:T(1,128)} %bitcast.30), channel_id=1, source_target_pairs={{0,8},{4,12},{8,0},{12,4},{1,9},{5,13},{9,1},{13,5},{2,10},{6,14},... | collective-permute-start | bytes 104 | tf_op jit(solution)/shard_map/ppermute | solution.py:438
  4.0 4.3 %collective-permute-start.171 = (s32[1,8]{1,0:T(1,128)}, s32[1,8]{1,0:T(1,128)S(1)}, u32[]{:S(2)}, u32[]{:S(2)}) collective-permute-start(s32[1,8]{1,0:T(1,128)} %bitcast.31), channel_id=1, source_target_pairs={{0,4},{4,8},{8,12},{12,0},{1,5},{5,9},{9,13},{13,1},{2,6},{6,10},{... | collective-permute-start | bytes 104 | tf_op jit(solution)/shard_map/ppermute | solution.py:438
  4.9 3.5 %copy-start.9 = (s32[1,8]{1,0:T(1,128)}, s32[1,8]{1,0:T(1,128)S(1)}, u32[]{:S(2)}) copy-start(s32[1,8]{1,0:T(1,128)S(1)} %collective-permute-done.173.refs_4_) | copy-start | bytes 100
  7.4 0.9 %copy-start.10 = (s32[1,8]{1,0:T(1,128)}, s32[1,8]{1,0:T(1,128)S(1)}, u32[]{:S(2)}) copy-start(s32[1,8]{1,0:T(1,128)S(1)} %collective-permute-done.172.refs_3_) | copy-start | bytes 100
  8.3 0.5 copy-start.11
  12.9 49.4 %copy-start.1 = (f32[40,1024]{1,0:T(8,128)S(1)}, f32[40,1024]{1,0:T(8,128)}, u32[]{:S(2)}) copy-start(f32[40,1024]{1,0:T(8,128)} %get-tuple-element.567.wide) | copy-start | bytes 491524
  12.9 49.4 %copy-start.2 = (f32[2,8,1280]{2,1,0:T(8,128)S(1)}, f32[2,8,1280]{2,1,0:T(8,128)}, u32[]{:S(2)}) copy-start(f32[2,8,1280]{2,1,0:T(8,128)} %get-tuple-element.569.begun) | copy-start | bytes 245764
  13.0 49.4 %copy-start.3 = (f32[2,8,1024]{2,1,0:T(8,128)S(1)}, f32[2,8,1024]{2,1,0:T(8,128)}, u32[]{:S(2)}) copy-start(f32[2,8,1024]{2,1,0:T(8,128)} %get-tuple-element.568.gate) | copy-start | bytes 196612
  13.0 49.4 %copy-start.4 = (bf16[4,1,1280]{2,0,1:T(4,128)(2,1)S(1)}, bf16[4,1,1280]{2,0,1:T(4,128)(2,1)}, u32[]{:S(2)}) copy-start(bf16[4,1,1280]{2,0,1:T(4,128)(2,1)} %param.113) | copy-start | bytes 30724
  13.0 49.4 %copy-start.6 = (f32[1,1024]{1,0:T(1,128)S(1)}, f32[1,1024]{1,0:T(1,128)}, u32[]{:S(2)}) copy-start(f32[1,1024]{1,0:T(1,128)} %get-tuple-element.570.norm_gain) | copy-start | bytes 12292
  13.0 49.4 %copy-start.7 = (s32[4]{0:T(128)S(1)}, s32[4]{0:T(128)}, u32[]{:S(2)}) copy-start(s32[4]{0:T(128)} %live.3) | copy-start | bytes 52
  13.0 49.4 %copy-start.8 = (s32[2]{0:T(128)S(1)}, s32[2]{0:T(128)}, u32[]{:S(2)}) copy-start(s32[2]{0:T(128)} %get-tuple-element.561.loops) | copy-start | bytes 28
  13.1 49.3 %collective-permute-start.42 = (bf16[4256,128]{1,0:T(8,128)(2,1)S(1)}, bf16[4256,128]{1,0:T(8,128)(2,1)}, u32[]{:S(2)}, u32[]{:S(2)}) collective-permute-start(bf16[4256,128]{1,0:T(8,128)(2,1)S(1)} %get-tuple-element.407), channel_id=1, source_target_pairs={{0,8},{4,12},{8,0},{12,4},{1,9},{5,13},{9,1},{13,5},{2,10},{6,14},... | collective-permute-start | bytes 3268616 | tf_op jit(solution)/shard_map/cond/branch_23_fun/ppermute | solution.py:491
  62.4 7.1 %copy-start = (bf16[2,8,1,1280]{3,1,2,0:T(8,128)(2,1)S(1)}, bf16[2,8,1,1280]{3,1,2,0:T(8,128)(2,1)}, u32[]{:S(2)}) copy-start(bf16[2,8,1,1280]{3,1,2,0:T(8,128)(2,1)} %param.110) | copy-start | bytes 122884
  62.4 7.1 %copy-start.5 = (f32[8,16]{1,0:T(8,128)S(1)}, f32[8,16]{1,0:T(8,128)}, u32[]{:S(2)}) copy-start(f32[8,16]{1,0:T(8,128)} %get-tuple-element.574.scale) | copy-start | bytes 1540
  67.2 6.1 %collective-permute-start.176 = (bf16[16,4096]{1,0:T(8,128)(2,1)S(1)}, bf16[16,4096]{1,0:T(8,128)(2,1)S(1)}, u32[]{:S(2)}, u32[]{:S(2)}) collective-permute-start(bf16[16,4096]{1,0:T(8,128)(2,1)S(1)} %get-tuple-element.571), channel_id=1, source_target_pairs={{0,3},{1,2},{2,1},{3,0},{4,7},{5,6},{6,5},{7,4},{8,11},{9,10},{10,... | collective-permute-start | bytes 393224 | tf_op jit(solution)/shard_map/ppermute | solution.py:536
  68.9 6.9 %collective-permute-start.175 = (bf16[16,4096]{1,0:T(8,128)(2,1)S(1)}, bf16[16,4096]{1,0:T(8,128)(2,1)S(1)}, u32[]{:S(2)}, u32[]{:S(2)}) collective-permute-start(bf16[16,4096]{1,0:T(8,128)(2,1)S(1)} %get-tuple-element.571), channel_id=1, source_target_pairs={{0,2},{1,3},{2,0},{3,1},{4,6},{5,7},{6,4},{7,5},{8,10},{9,11},{10,... | collective-permute-start | bytes 393224 | tf_op jit(solution)/shard_map/ppermute | solution.py:536
  69.1 6.7 %collective-permute-start.174 = (bf16[16,4096]{1,0:T(8,128)(2,1)S(1)}, bf16[16,4096]{1,0:T(8,128)(2,1)S(1)}, u32[]{:S(2)}, u32[]{:S(2)}) collective-permute-start(bf16[16,4096]{1,0:T(8,128)(2,1)S(1)} %get-tuple-element.571), channel_id=1, source_target_pairs={{0,1},{1,0},{2,3},{3,2},{4,5},{5,4},{6,7},{7,6},{8,9},{9,8},{10,11... | collective-permute-start | bytes 393224 | tf_op jit(solution)/shard_map/ppermute | solution.py:536
